TPU v7x, 32 devices: a whole 2x2x4 slice. The times are simulated.
32 devices in a mesh: space: 8 (over z, x), vel: 4 (over y, core).
Axes of the slice: x: 2, y: 2, z: 4, core: 2. Of those that a mesh axis runs over, the one named last changes fastest.
Arguments:
- populations: float32 [64, 512, 2048], P('vel', 'space'), may hold values from 0.2 to 41, as said below
- shift_x: int32 [64], P('vel'), may hold values from -8 to 8, as said below
- shift_y: int32 [64], P('vel'), may hold values from -8 to 8, as said below
- frac_x: float32 [64], P('vel'), may hold values from 0 to 1
- frac_y: float32 [64], P('vel'), may hold values from 0 to 1
- inflow: float32 [64], P('vel'), may hold values from 0.5 to 2
- wall_state: float32 [64], P('vel'), may hold values from 0.5 to 2
- heights: int32 [2048], replicated, may hold values from 0 to 128
- impact_frequency_factor: float32 [], replicated, may hold values from 0.5 to 2
Outputs:
- relaxed: float32 [64, 512, 2048], P('vel', 'space')
Inputs may be any that keep to these rules, and one draw needn't show every extreme that they name: `populations`: positive. `shift_x`: the values -8 and 8 both occur. `shift_y`: the values -8 and 8 both occur.
All inputs are finite; a program needn't handle non-finite values.
Results may differ from a plain program's by a relative error of at most 0.00002.
Values sent between devices are 32-bit elements; how exact they have to be, the bound alone decides.
No kernel may reach another device: no remote copies, remote signals or barrier semaphores. Data moves between devices by JAX's collectives and lax.ppermute only.
A program may use at most 128 MiB of HBM per device.

v0:
```python
import functools
import math

import jax
import jax.numpy as jnp
from jax import lax
from jax.experimental import pallas as pl
from jax.experimental.pallas import tpu as pltpu
from jax.sharding import PartitionSpec as P

SPEED_TALLY = 64
CFL = 8
LOW_ROWS = CFL + 1
HIGH_ROWS = CFL
ROW = 8
LANE = 128
PAD = 16
F32 = jnp.float32
LOW_SENT = 80
HIGH_SENT = 64

SMEM_SPEC = pl.BlockSpec(memory_space=pltpu.SMEM)
ANY_SPEC = pl.BlockSpec(memory_space=pl.ANY)
HBM_SPEC = pl.BlockSpec(memory_space=pltpu.HBM)
VMEM_SPEC = pl.BlockSpec(memory_space=pltpu.VMEM)


def params(mebibytes):
    return pltpu.CompilerParams(vmem_limit_bytes=mebibytes * 1024 * 1024)


def in_hbm(*arrays):
    return [pltpu.with_memory_space_constraint(x, pltpu.HBM) for x in arrays]


def place(rows):
    space = lax.axis_index("space")
    return space * rows, space == 0, space == lax.axis_size("space") - 1, lax.axis_index("vel") % 2


def low_need(shift):
    return jnp.where(shift >= 0, shift + 1, 0)


def high_need(shift):
    return jnp.where(shift < 0, -shift, 0)


def fill_rows(padded, v, columns, start, count, value):
    block = jnp.full((ROW, LANE), value, F32)
    for t in columns:
        for r in range(start, start + count, ROW):
            padded[v, t, r : r + ROW, :] = block


def prepare_heights(heights_ref, bars):
    lane_tiles = heights_ref.shape[0]
    sublane = lax.broadcasted_iota(jnp.int32, (ROW, LANE), 0)
    for t in range(lane_tiles):
        bars[t] = jnp.broadcast_to(heights_ref[t : t + 1, :], (ROW, LANE)) - sublane


def advect(padded, v, scalars, tiles):
    sx, sy, fx, fy = scalars
    lane_tiles = padded.shape[1] - 2
    lane = lax.broadcasted_iota(jnp.int32, (ROW, LANE), 1)
    near_roll = jnp.where(sx < 0, sx + LANE, sx)
    far_roll = jnp.where(sx + 1 < 0, sx + 1 + LANE, sx + 1)

    def moved(start, t):
        nearer = padded[v, t + 1, pl.ds(start, ROW), :]
        further = padded[v, t + 1, pl.ds(start - 1, ROW), :]
        line = (1.0 - fy) * nearer + fy * further
        if t < 0 or t == lane_tiles:
            return line, line
        return pltpu.roll(line, near_roll, 1), pltpu.roll(line, far_roll, 1)

    def blend(put, t, near, far):
        put(t, (1.0 - fx) * near + fx * far)

    @pl.when(sx >= 0)
    def _():
        own_near, own_far = lane >= sx, lane >= sx + 1
        for begin, put in tiles:
            before = moved(begin - sy, -1)
            for t in range(lane_tiles):
                here = moved(begin - sy, t)
                near = jnp.where(own_near, here[0], before[0])
                blend(put, t, near, jnp.where(own_far, here[1], before[1]))
                before = here

    @pl.when(sx < 0)
    def _():
        own_near, own_far = lane < sx + LANE, lane < sx + 1 + LANE
        for begin, put in tiles:
            here = moved(begin - sy, 0)
            for t in range(lane_tiles):
                after = moved(begin - sy, t + 1)
                near = jnp.where(own_near, here[0], after[0])
                blend(put, t, near, jnp.where(own_far, here[1], after[1]))
                here = after


def store_masked(target, bars, first_row, solid_value):
    def put(t, value):
        target[t] = jnp.where(first_row < bars[t], solid_value, value)

    return put


def velocity(sx_ref, sy_ref, fx_ref, fy_ref, v):
    return sx_ref[v].astype(F32) + fx_ref[v], sy_ref[v].astype(F32) + fy_ref[v]


def sum_moments(planes_ref, k, weights, lane_tile_range):
    sums = [[None] * 4 for _ in lane_tile_range]
    for v, (along_x, along_y) in enumerate(weights):
        square = along_x * along_x + along_y * along_y
        for n, t in enumerate(lane_tile_range):
            f = planes_ref[v, k, t]
            terms = (f, f * along_x, f * along_y, f * square)
            sums[n] = [b if a is None else a + b for a, b in zip(sums[n], terms)]
    return sums


class Plan:
    def __init__(self, row_tiles, half):
        self.tile = 4 * half
        self.inside = list(range(2, row_tiles - 2))
        self.sizes = [self.tile + 4, self.tile, len(self.inside) * self.tile, 2 * self.tile, 2 * self.tile]
        self.starts = [sum(self.sizes[:n]) for n in range(len(self.sizes) + 1)]
        self.row_tiles = row_tiles

    def start(self, j):
        low = self.starts[3] + self.tile * j
        high = self.starts[4] + self.tile * (j - self.row_tiles + 2)
        inside = self.starts[2] + self.tile * (j - 2)
        return jnp.where(j < 2, low, jnp.where(j >= self.row_tiles - 2, high, inside))


def advance_kernel(plan, cuts, group, sx_ref, sy_ref, fx_ref, fy_ref, inflow_ref, wall_ref,
                   heights_ref, pop_ref, *refs):
    planes_ref, mine_ref, theirs_ref, more_ref = refs[:4]
    packs = refs[4 : 4 + len(cuts)]
    (padded, planes_buf, outer, last_row, low_pack, high_pack, bars, sem_in, sem_planes, sem_out) = refs[
        4 + len(cuts) :
    ]
    planes, row_tiles, lane_tiles = pop_ref.shape[:3]
    half = lane_tiles // 2
    rows = row_tiles * ROW
    row0, first, last, core = place(rows)

    def loads(g):
        members = pl.ds(g * group, group)
        return [
            pltpu.make_async_copy(
                pop_ref.at[members, i],
                padded.at[members, 1 : 1 + lane_tiles, PAD + ROW * i : PAD + ROW * (i + 1), :],
                sem_in.at[g, i],
            )
            for i in range(row_tiles)
        ]

    def start(g, _):
        for load in loads(g):
            load.start()
        return 0

    lax.fori_loop(0, planes // group, start, 0)
    prepare_heights(heights_ref, bars)
    last_row[...] = jnp.zeros_like(last_row)

    def put_sums(h, first_block, sums):
        for is_mine, ref in ((True, mine_ref), (False, theirs_ref)):

            @pl.when((core == h) == is_mine)
            def _():
                for n, value in enumerate(sums):
                    ref[first_block + n] = value


    def out_copy(v):
        return pltpu.make_async_copy(planes_buf.at[v], planes_ref.at[v], sem_planes.at[v])

    def one(v, offsets):
        low, high = offsets
        value = inflow_ref[v]
        shift = sy_ref[v]
        up = shift >= 0
        columns = range(lane_tiles + 2)
        fill_rows(padded, v, (0, lane_tiles + 1), PAD, rows, value)
        fill_rows(padded, v, columns, 0, PAD, jnp.where(first, value, 0.0))
        fill_rows(padded, v, columns, PAD + rows, ROW, jnp.where(last, value, 0.0))

        @pl.when(v % group == 0)
        def _():
            for load in loads(v // group):
                load.wait()

        scalars = sx_ref[v], shift, fx_ref[v], fy_ref[v]
        work = [
            (PAD + ROW * j, store_masked(planes_buf.at[v, j], bars, row0 + ROW * j, wall_ref[v]))
            for j in range(row_tiles)
        ]
        beyond = jnp.where(up, rows, -ROW)
        work.append((PAD + beyond, store_masked(outer.at[v], bars, row0 + beyond, 0.0)))
        advect(padded, v, scalars, work)
        out_copy(v).start()

        @pl.when(shift == CFL)
        def _():
            along_x, along_y = velocity(sx_ref, sy_ref, fx_ref, fy_ref, v)
            factors = 1.0, along_x, along_y, along_x * along_x + along_y * along_y

            def put(t, value):
                row = jnp.where(row0 + rows + ROW < bars[t], 0.0, value)
                h, r = divmod(t, half)
                for m in range(4):
                    total = last_row[h, m, r : r + 1, :] + (row * factors[m])[0:1, :]
                    last_row[h, m, r : r + 1, :] = total

            advect(padded, v, scalars, [(PAD + rows + ROW, put)])

        @pl.when(up)
        def _():
            for t in range(lane_tiles):
                source = pl.ds(PAD + rows - 1 - shift, 8)
                low_pack[t, pl.ds(low, 8), :] = padded[v, t + 1, source, :]

        @pl.when(shift == CFL)
        def _():
            for t in range(lane_tiles):
                low_pack[t, pl.ds(low + 8, 1), :] = padded[v, t + 1, PAD + rows - 1 : PAD + rows, :]

        @pl.when(jnp.logical_not(up))
        def _():
            for t in range(lane_tiles):
                high_pack[t, pl.ds(high, 8), :] = padded[v, t + 1, PAD : PAD + 8, :]

        return low + low_need(shift), high + high_need(shift)

    needs = lax.fori_loop(0, planes, one, (jnp.int32(0), jnp.int32(0)))
    sent = [end for _, begin, end in cuts if begin == 0]
    overflows = (needs[0] > sent[0]) | (needs[1] > sent[1])
    more_ref[0] = jnp.where(overflows, 1, 0)

    def pack_copy(n):
        pack, begin, end = cuts[n]
        source = (low_pack, high_pack)[pack].at[:, begin:end, :]
        return pltpu.make_async_copy(source, packs[n], sem_out.at[n])

    def each_pack(act):
        for n, (_, begin, _) in enumerate(cuts):
            if begin == 0:
                act(pack_copy(n))
            else:
                pl.when(overflows)(lambda n=n: act(pack_copy(n)))

    each_pack(lambda copy: copy.start())
    for h in range(2):
        put_sums(h, plan.tile, [last_row[h, m] for m in range(4)])
        for rising in (True, False):
            for part in range(2):
                tiles = range(h * half + part * half // 2, h * half + (part + 1) * half // 2)
                sums = [[None] * 4 for _ in tiles]
                for v in range(planes):
                    along_x, along_y = velocity(sx_ref, sy_ref, fx_ref, fy_ref, v)
                    goes = jnp.where((sy_ref[v] >= 0) == rising, 1.0, 0.0)
                    square = (along_x * along_x + along_y * along_y) * goes
                    factors = goes, along_x * goes, along_y * goes, square
                    for n, t in enumerate(tiles):
                        f = outer[v, t]
                        terms = [f * w for w in factors]
                        sums[n] = [b if a is None else a + b for a, b in zip(sums[n], terms)]
                begin = plan.starts[0 if rising else 1] + part * half // 2
                for m in range(4):
                    put_sums(h, begin + m * half, [sums[n][m] for n in range(len(tiles))])
    weights = [velocity(sx_ref, sy_ref, fx_ref, fy_ref, v) for v in range(planes)]

    def step(j, _):
        begin = plan.start(j)
        for h in range(2):
            sums = sum_moments(planes_buf, j, weights, range(h * half, (h + 1) * half))
            put_sums(h, begin, [sums[t][m] for m in range(4) for t in range(half)])
        return 0

    lax.fori_loop(0, row_tiles, step, 0)

    def finish(v, _):
        out_copy(v).wait()
        return 0

    lax.fori_loop(0, planes, finish, 0)
    each_pack(lambda copy: copy.wait())


def advance(plan, small, heights, pop, cuts):
    planes, row_tiles, lane_tiles = pop.shape[:3]
    group = math.gcd(planes, 2)
    blocks = plan.starts[-1]
    half_sums = jax.ShapeDtypeStruct((blocks, ROW, LANE), F32)
    return pl.pallas_call(
        functools.partial(advance_kernel, plan, cuts, group),
        out_shape=[pltpu.HBM(pop.shape, F32), half_sums, half_sums, jax.ShapeDtypeStruct((1,), jnp.int32)]
        + [pltpu.HBM((lane_tiles, end - begin, LANE), F32) for _, begin, end in cuts],
        in_specs=[SMEM_SPEC] * 6 + [VMEM_SPEC, HBM_SPEC],
        out_specs=[HBM_SPEC, VMEM_SPEC, VMEM_SPEC, SMEM_SPEC] + [HBM_SPEC] * len(cuts),
        scratch_shapes=[
            pltpu.VMEM((planes, lane_tiles + 2, PAD + row_tiles * ROW + ROW, LANE), F32),
            pltpu.VMEM((planes, row_tiles, lane_tiles, ROW, LANE), F32),
            pltpu.VMEM((planes, lane_tiles, ROW, LANE), F32),
            pltpu.VMEM((2, 4, ROW, LANE), F32),
            pltpu.VMEM((lane_tiles, planes * LOW_ROWS + 16, LANE), F32),
            pltpu.VMEM((lane_tiles, planes * HIGH_ROWS + 16, LANE), F32),
            pltpu.VMEM((lane_tiles, ROW, LANE), jnp.int32),
            pltpu.SemaphoreType.DMA((planes // group, row_tiles)),
            pltpu.SemaphoreType.DMA((planes,)),
            pltpu.SemaphoreType.DMA((len(cuts),)),
        ],
        compiler_params=params(36),
        name="advance",
    )(*in_hbm(*small, heights, pop))


def fold_kernel(mine_ref, received_ref, *out_refs):
    begin = 0
    for ref in out_refs:
        n = ref.shape[0]
        ref[...] = mine_ref[begin : begin + n] + received_ref[begin : begin + n]
        begin += n


def fold(mine, received, sizes):
    return pl.pallas_call(
        fold_kernel,
        out_shape=[jax.ShapeDtypeStruct((n, ROW, LANE), F32) for n in sizes],
        in_specs=[VMEM_SPEC] * 2,
        out_specs=[VMEM_SPEC] * len(sizes),
        compiler_params=params(8),
        name="fold",
    )(mine, received)


def join_low_kernel(own_ref, low_ref, *refs):
    out_ref = refs[-1]
    tile = own_ref.shape[0] // 2
    half = tile // 4
    out_ref[2 * tile :] = jnp.zeros((out_ref.shape[0] - 2 * tile, ROW, LANE), F32)
    out_ref[:tile] = own_ref[:tile] + low_ref[:tile]
    top = lax.broadcasted_iota(jnp.int32, (ROW, LANE), 0) == 0
    for m in range(4):
        for n in range(half):
            row = jnp.broadcast_to(low_ref[tile + m, n : n + 1, :], (ROW, LANE))
            index = tile + m * half + n
            out_ref[index] = own_ref[index] + jnp.where(top, row, 0.0)


def add_kernel(a_ref, b_ref, *refs):
    refs[-1][...] = a_ref[...] + b_ref[...]


def join_high_kernel(own_ref, high_ref, *refs):
    out_ref = refs[-1]
    tile = high_ref.shape[0]
    out_ref[2 * tile :] = jnp.zeros((out_ref.shape[0] - 2 * tile, ROW, LANE), F32)
    out_ref[:tile] = own_ref[:tile]
    out_ref[tile : 2 * tile] = own_ref[tile:] + high_ref[...]


def small_call(kernel, name, a, b, after=(), extra=0):
    operands = a, b, *after
    shape = (a.shape[0] + extra, *a.shape[1:])
    return pl.pallas_call(
        kernel,
        out_shape=jax.ShapeDtypeStruct(shape, F32),
        in_specs=[VMEM_SPEC] * 2 + [ANY_SPEC] * len(after),
        out_specs=VMEM_SPEC,
        compiler_params=params(8),
        name=name,
    )(*operands)


def profile(density, flux_x, flux_y, energy, factor):
    inverse = 1.0 / density
    mean_x = flux_x * inverse
    mean_y = flux_y * inverse
    temperature = 0.5 * (energy * inverse - mean_x * mean_x - mean_y * mean_y)
    rate = 1.0 - jnp.exp(-factor * density / (SPEED_TALLY * jnp.sqrt(temperature)))
    height = rate * (density / (2.0 * math.pi * temperature))
    return mean_x, mean_y, -0.5 / temperature, height, 1.0 - rate


def relax_cells(get, put, values, factor, weights):
    mean_x, mean_y, scale, height, keep = profile(*values, factor)
    for v, (along_x, along_y) in enumerate(weights):
        gap_x = along_x - mean_x
        gap_y = along_y - mean_y
        state = height * jnp.exp((gap_x * gap_x + gap_y * gap_y) * scale)
        put(v, keep * get(v) + state)


def relax_tile(buf, sums, base, core, factor, weights, k, h):
    mine_ref, other_ref = sums
    half = buf.shape[2] // 2
    for n in range(half):
        t = h * half + n
        values = []
        for m in range(4):
            index = base + m * half + n
            values.append(jnp.where(core == h, mine_ref[index], other_ref[index]))

        def put(v, value):
            buf[v, k, t] = value

        relax_cells(lambda v: buf[v, k, t], put, values, factor, weights)


def relax_kernel(sizes, meta_ref, sx_ref, sy_ref, fx_ref, fy_ref, factor_ref, planes_ref, *refs):
    sums_refs = refs[:-4]
    out_ref, buf, sem_in, sem_out = refs[-4:]
    planes, row_tiles, lane_tiles = planes_ref.shape[:3]
    half = lane_tiles // 2

    def copy(j, h, out):
        lanes = pl.ds(h * half, half)
        here = buf.at[:, j, lanes]
        if out:
            return pltpu.make_async_copy(here, out_ref.at[:, j, lanes], sem_out.at[2 * j + h])
        return pltpu.make_async_copy(planes_ref.at[:, j, lanes], here, sem_in.at[2 * j + h])

    def tile(k):
        return jnp.where(k < row_tiles - 2, k + 2, k + 2 - row_tiles)

    def start(k, _):
        for h in range(2):
            copy(tile(k), h, False).start()
        return 0

    lax.fori_loop(0, row_tiles, start, 0)
    weights = [velocity(sx_ref, sy_ref, fx_ref, fy_ref, v) for v in range(planes)]
    begin = 0
    for pair, size in enumerate(sizes):
        sums = sums_refs[2 * pair : 2 * pair + 2]

        def step(k, _, begin=begin, sums=sums):
            j = tile(k)
            for h in range(2):
                copy(j, h, False).wait()
                base = (k - begin) * 4 * half
                relax_tile(buf, sums, base, meta_ref[3], factor_ref[0], weights, j, h)
                copy(j, h, True).start()
            return 0

        lax.fori_loop(begin, begin + size, step, 0)
        begin += size

    def finish(j, _):
        for h in range(2):
            copy(j, h, True).wait()
        return 0

    lax.fori_loop(0, row_tiles, finish, 0)


def relax_all(sizes, meta, small, factor, sums, moved):
    planes, row_tiles, lane_tiles = moved.shape[:3]
    operands = [*in_hbm(meta, *small[:4]), factor, *in_hbm(moved), *sums]
    return pl.pallas_call(
        functools.partial(relax_kernel, sizes),
        out_shape=pltpu.HBM(moved.shape, F32),
        in_specs=[SMEM_SPEC] * 6 + [HBM_SPEC] + [VMEM_SPEC] * len(sums),
        out_specs=HBM_SPEC,
        scratch_shapes=[
            pltpu.VMEM((planes, row_tiles, lane_tiles, ROW, LANE), F32),
            pltpu.SemaphoreType.DMA((2 * row_tiles,)),
            pltpu.SemaphoreType.DMA((2 * row_tiles,)),
        ],
        compiler_params=params(24),
        name="relax_all",
    )(*operands)


def finish_kernel(cuts, meta_ref, sx_ref, sy_ref, fx_ref, fy_ref, inflow_ref, factor_ref, heights_ref,
                  m_low, o_low, m_high, o_high, before_ref, *refs):
    pack_refs = refs[: len(cuts)]
    out_ref, frames, buf, keeps, low_buf, high_buf, bars, sem_in, sem_planes, sem_out = refs[len(cuts) :]
    planes, row_tiles, lane_tiles = before_ref.shape[:3]
    half = lane_tiles // 2
    row0, first, last, core = (meta_ref[i] for i in range(4))
    needs = [low_need(sy_ref[0]), high_need(sy_ref[0])]
    for v in range(1, planes):
        needs = [needs[0] + low_need(sy_ref[v]), needs[1] + high_need(sy_ref[v])]

    def pack_copy(n):
        pack, begin, end = cuts[n]
        target = (low_buf, high_buf)[pack].at[:, 16 + begin : 16 + end, :]
        return pltpu.make_async_copy(pack_refs[n], target, sem_in.at[n])

    def cases(v):
        shift = sy_ref[v]
        from_low = (shift >= 0) & (first == 0)
        return from_low, (shift < 0) & (last == 0), from_low & (shift == CFL)

    tile_of = 0, row_tiles - 1, 1
    slot_of = 0, 0, 1

    def copy(v, case, out):
        here = buf.at[v, slot_of[case]]
        if out:
            return pltpu.make_async_copy(here, out_ref.at[v, tile_of[case]], sem_out.at[v, slot_of[case]])
        there = before_ref.at[v, tile_of[case]]
        return pltpu.make_async_copy(there, here, sem_planes.at[v, slot_of[case]])

    for n in range(len(cuts)):
        pl.when(needs[cuts[n][0]] > cuts[n][1])(lambda n=n: pack_copy(n).start())

    def start(v, _):
        for case, applies in enumerate(cases(v)):
            pl.when(applies)(lambda case=case: copy(v, case, False).start())
        return 0

    lax.fori_loop(0, planes, start, 0)
    prepare_heights(heights_ref, bars)
    for t in range(lane_tiles + 2):
        for r in (24, 32):
            frames[0, t, r : r + ROW, :] = jnp.zeros((ROW, LANE), F32)
        for r in (16, 24):
            frames[1, t, r : r + ROW, :] = jnp.zeros((ROW, LANE), F32)
    edges = ((m_low, o_low), 0), ((m_high, o_high), 4 * half), ((m_low, o_low), 4 * half)
    for case, (sums, base) in enumerate(edges):
        for t in range(lane_tiles):
            h, n = divmod(t, half)
            values = []
            for m in range(4):
                index = base + m * half + n
                values.append(jnp.where(core == h, sums[0][index], sums[1][index]))
            keeps[case, t] = profile(*values, factor_ref[0])[4]
    for n in range(len(cuts)):
        pl.when(needs[cuts[n][0]] > cuts[n][1])(lambda n=n: pack_copy(n).wait())

    def add_masked(v, case):
        first_row = row0 + ROW * tile_of[case]

        def put(t, value):
            part = jnp.where(first_row < bars[t], 0.0, value)
            buf[v, slot_of[case], t] = buf[v, slot_of[case], t] + keeps[case, t] * part

        return put

    def one(v, offsets):
        low, high = offsets
        value = inflow_ref[v]
        shift = sy_ref[v]
        scalars = sx_ref[v], shift, fx_ref[v], fy_ref[v]
        borders = (0, lane_tiles + 1)
        from_low, from_high, reaches_second = cases(v)

        @pl.when(from_low)
        def _():
            fill_rows(frames, 0, borders, 8, 16, value)
            for t in range(lane_tiles):
                for r in range(0, 16, ROW):
                    piece = low_buf[t, pl.ds(low + shift + 1 + r, ROW), :]
                    frames[0, t + 1, 8 + r : 8 + r + ROW, :] = piece
            copy(v, 0, False).wait()
            advect(frames, 0, scalars, [(24, add_masked(v, 0))])
            copy(v, 0, True).start()

        @pl.when(reaches_second)
        def _():
            copy(v, 2, False).wait()
            advect(frames, 0, scalars, [(32, add_masked(v, 2))])
            copy(v, 2, True).start()

        @pl.when(from_high)
        def _():
            fill_rows(frames, 1, borders, 32, 8, value)
            for t in range(lane_tiles):
                frames[1, t + 1, 32:40, :] = high_buf[t, pl.ds(16 + high, ROW), :]
            copy(v, 1, False).wait()
            advect(frames, 1, scalars, [(24, add_masked(v, 1))])
            copy(v, 1, True).start()

        return low + low_need(shift), high + high_need(shift)

    lax.fori_loop(0, planes, one, (jnp.int32(0), jnp.int32(0)))

    def end(v, _):
        for case, applies in enumerate(cases(v)):
            pl.when(applies)(lambda case=case: copy(v, case, True).wait())
        return 0

    lax.fori_loop(0, planes, end, 0)


def finish_edges(meta, small, factor, heights, sums, packs, cuts, out):
    planes, _, lane_tiles = out.shape[:3]
    fixed = [*in_hbm(meta, *small[:5]), factor, *in_hbm(heights)]
    operands = [*fixed, *sums, *in_hbm(out), *packs]
    return pl.pallas_call(
        functools.partial(finish_kernel, cuts),
        out_shape=pltpu.HBM(out.shape, F32),
        in_specs=[SMEM_SPEC] * 7 + [VMEM_SPEC] * 5 + [HBM_SPEC] + [ANY_SPEC] * len(cuts),
        out_specs=HBM_SPEC,
        scratch_shapes=[
            pltpu.VMEM((2, lane_tiles + 2, 48, LANE), F32),
            pltpu.VMEM((planes, 2, lane_tiles, ROW, LANE), F32),
            pltpu.VMEM((3, lane_tiles, ROW, LANE), F32),
            pltpu.VMEM((lane_tiles, planes * LOW_ROWS + 32, LANE), F32),
            pltpu.VMEM((lane_tiles, planes * HIGH_ROWS + 32, LANE), F32),
            pltpu.VMEM((lane_tiles, ROW, LANE), jnp.int32),
            pltpu.SemaphoreType.DMA((len(cuts),)),
            pltpu.SemaphoreType.DMA((planes, 2)),
            pltpu.SemaphoreType.DMA((planes, 2)),
        ],
        input_output_aliases={len(fixed) + len(sums): 0},
        compiler_params=params(24),
        name="finish_edges",
    )(*operands)


def per_device(populations, shift_x, shift_y, frac_x, frac_y, inflow, wall_state, heights,
               impact_frequency_factor):
    planes, row_count, col_count = populations.shape
    space_count, vel_count = lax.axis_size("space"), lax.axis_size("vel")
    row_tiles, lane_tiles = row_count // ROW, col_count // LANE
    space, vel = lax.axis_index("space"), lax.axis_index("vel")
    forward = [(i, i + 1) for i in range(space_count - 1)]
    backward = [(target, source) for source, target in forward]
    partner = [(i, i ^ 1) for i in range(vel_count)]
    across = [(i, i ^ 2) for i in range(vel_count)]

    meta = jnp.stack([space * row_count, space == 0, space == space_count - 1, vel % 2]).astype(jnp.int32)
    small = (shift_x, shift_y, frac_x, frac_y, inflow, wall_state)
    factor = impact_frequency_factor.reshape(1)
    bars = heights.reshape(lane_tiles, LANE)
    pop = populations.reshape(planes, row_tiles, ROW, lane_tiles, LANE).transpose(0, 1, 3, 2, 4)
    low_sent, high_sent = min(LOW_SENT, planes * LOW_ROWS), min(HIGH_SENT, planes * HIGH_ROWS)
    cuts = [
        (0, 0, low_sent),
        (1, 0, high_sent),
        (0, low_sent, planes * LOW_ROWS),
        (1, high_sent, planes * HIGH_ROWS),
    ]
    plan = Plan(row_tiles, lane_tiles // 2)

    moved, mine, theirs, more_needed, *packs = advance(plan, small, bars, pop, cuts)
    received = lax.ppermute(theirs, "vel", partner)
    up, down, inside, edge_low, edge_high = fold(mine, received, plan.sizes)
    from_low = lax.ppermute(up, "space", forward)
    from_high = lax.ppermute(down, "space", backward)
    low_first = lax.ppermute(packs[0], "space", forward)
    high_first = lax.ppermute(packs[1], "space", backward)

    def total(sums, after=()):
        whole = small_call(add_kernel, "add", sums, lax.ppermute(sums, "vel", across), after)
        return whole, lax.ppermute(whole, "vel", partner)

    def send_more(low, high):
        return lax.ppermute(low, "space", forward), lax.ppermute(high, "space", backward)

    more = lax.cond(more_needed[0] > 0, send_more, lambda low, high: (low, high), packs[2], packs[3])
    sums_inside = total(inside)
    sums_low = total(small_call(join_low_kernel, "join_low", edge_low, from_low, (), 1))
    sums_high = total(small_call(join_high_kernel, "join_high", edge_high, from_high, (), 1))
    sizes = len(plan.inside), 2, 2
    out = relax_all(sizes, meta, small, factor, sums_inside + sums_high + sums_low, moved)
    halo = low_first, high_first, *more
    out = finish_edges(meta, small, factor, bars, sums_low + sums_high, halo, cuts, out)
    return out.transpose(0, 1, 3, 2, 4).reshape(planes, row_count, col_count)


def solution(mesh):
    return jax.shard_map(
        per_device,
        mesh=mesh,
        in_specs=(
            P("vel", "space", None),
            P("vel"),
            P("vel"),
            P("vel"),
            P("vel"),
            P("vel"),
            P("vel"),
            P(),
            P(),
        ),
        out_specs=P("vel", "space", None),
        check_vma=False,
    )
```

profile of v0, /device:TPU:9, one launch (start us, length us, event | category | flops | bytes accessed | tf_op | source)
XLA Modules:
  0.0 62.1 jit_solution(3031406578001246532)
XLA Ops:
  0.0 14.0 %advance.1 = (f32[16,8,16,8,128]{4,3,2,1,0:T(8,128)}, f32[324,8,128]{2,1,0:T(8,128)S(1)}, f32[324,8,128]{2,1,0:T(8,128)S(1)}, s32[1]{0:T(128)}, f32[16,80,128]{2...) custom-call(s32[16]{0:T(128)} %sx_ref.5, s32[16]{0:T(128)} %sy_ref.5, ...), custom_call_target="tpu_custom_call" | custom-call | tf_op jit(solution)/shard_map/advance/pallas_call | solution.py:302
  14.0 0.7 %collective-permute-start.2 = (f32[324,8,128]{2,1,0:T(8,128)S(1)}, f32[324,8,128]{2,1,0:T(8,128)S(1)}, u32[]{:S(2)}, u32[]{:S(2)}) collective-permute-start(f32[324,8,128]{2,1,0:T(8,128)S(1)} %get-tuple-element.31), channel_id=1, source_target_pairs={{0,1},{1,0},{2,3},{3,2},{4,5},{5,4},{6,7},{7,6},{8,9},{9,8},{10,11... | collective-permute-start | bytes 3981320 | tf_op jit(solution)/shard_map/ppermute | solution.py:648
  14.7 2.7 %collective-permute-done.2.received_ref = f32[324,8,128]{2,1,0:T(8,128)S(1)} collective-permute-done((f32[324,8,128]{2,1,0:T(8,128)S(1)}, f32[324,8,128]{2,1,0:T(8,128)S(1)}, u32[]{:S(2)}, u32[]{:S(2)}) %collective-permute-start.2) | collective-permute-done | bytes 1327136 | tf_op jit(solution)/shard_map/ppermute | solution.py:648
  17.4 0.1 fold.1
  17.6 1.2 %collective-permute-start.9 = (f32[128,8,128]{2,1,0:T(8,128)S(1)}, f32[128,8,128]{2,1,0:T(8,128)S(1)}, u32[]{:S(2)}, u32[]{:S(2)}) collective-permute-start(f32[128,8,128]{2,1,0:T(8,128)S(1)} %get-tuple-element.37.a_ref), channel_id=1, source_target_pairs={{0,2},{1,3},{2,0},{3,1},{4,6},{5,7},{6,4},{7,5},{8,10},{9,11},{10,... | collective-permute-start | bytes 1572872 | tf_op jit(solution)/shard_map/ppermute | solution.py:656
  18.7 3.1 %collective-permute-start.3 = (f32[36,8,128]{2,1,0:T(8,128)S(1)}, f32[36,8,128]{2,1,0:T(8,128)S(1)}, u32[]{:S(2)}, u32[]{:S(2)}) collective-permute-start(f32[36,8,128]{2,1,0:T(8,128)S(1)} %get-tuple-element.33), channel_id=1, source_target_pairs={{0,4},{4,8},{8,12},{12,16},{16,20},{20,24},{24,28},{1,5},{5,9},{9,... | collective-permute-start | bytes 442376 | tf_op jit(solution)/shard_map/ppermute | solution.py:650
  21.8 3.1 %collective-permute-start.6 = (f32[32,8,128]{2,1,0:T(8,128)S(1)}, f32[32,8,128]{2,1,0:T(8,128)S(1)}, u32[]{:S(2)}, u32[]{:S(2)}) collective-permute-start(f32[32,8,128]{2,1,0:T(8,128)S(1)} %get-tuple-element.35), channel_id=1, source_target_pairs={{4,0},{8,4},{12,8},{16,12},{20,16},{24,20},{28,24},{5,1},{9,5},{13... | collective-permute-start | bytes 393224 | tf_op jit(solution)/shard_map/ppermute | solution.py:651
  25.6 2.2 %collective-permute-start.11 = (f32[16,80,128]{2,1,0:T(8,128)}, f32[16,80,128]{2,1,0:T(8,128)S(1)}, u32[]{:S(2)}, u32[]{:S(2)}) collective-permute-start(f32[16,80,128]{2,1,0:T(8,128)} %get-tuple-element.38), channel_id=1, source_target_pairs={{0,4},{4,8},{8,12},{12,16},{16,20},{20,24},{24,28},{1,5},{5,9},{9,... | collective-permute-start | bytes 1966088 | tf_op jit(solution)/shard_map/ppermute | solution.py:652
  27.8 1.9 %collective-permute-done.6.high_ref = f32[32,8,128]{2,1,0:T(8,128)S(1)} collective-permute-done((f32[32,8,128]{2,1,0:T(8,128)S(1)}, f32[32,8,128]{2,1,0:T(8,128)S(1)}, u32[]{:S(2)}, u32[]{:S(2)}) %collective-permute-start.6) | collective-permute-done | bytes 131104 | tf_op jit(solution)/shard_map/ppermute | solution.py:651
  29.7 0.4 collective-permute-start.7
  30.1 0.0 collective-permute-done.3.low_ref
  30.2 1.2 %collective-permute-start.4 = (f32[65,8,128]{2,1,0:T(8,128)S(1)}, f32[65,8,128]{2,1,0:T(8,128)S(1)}, u32[]{:S(2)}, u32[]{:S(2)}) collective-permute-start(f32[65,8,128]{2,1,0:T(8,128)S(1)} %join_low.1.a_ref), channel_id=1, source_target_pairs={{0,2},{1,3},{2,0},{3,1},{4,6},{5,7},{6,4},{7,5},{8,10},{9,11},{10,... | collective-permute-start | bytes 798728 | tf_op jit(solution)/shard_map/ppermute | solution.py:656
  31.3 0.0 collective-permute-done.9.b_ref
  31.3 0.1 add.16.refs_0_
  31.4 1.5 %collective-permute-start.10 = (f32[128,8,128]{2,1,0:T(8,128)S(1)}, f32[128,8,128]{2,1,0:T(8,128)S(1)}, u32[]{:S(2)}, u32[]{:S(2)}) collective-permute-start(f32[128,8,128]{2,1,0:T(8,128)S(1)} %add.16.refs_0_), channel_id=1, source_target_pairs={{0,1},{1,0},{2,3},{3,2},{4,5},{5,4},{6,7},{7,6},{8,9},{9,8},{10,11... | collective-permute-start | bytes 1572872 | tf_op jit(solution)/shard_map/ppermute | solution.py:657
  33.0 3.1 %collective-permute-start.12 = (f32[16,64,128]{2,1,0:T(8,128)}, f32[16,64,128]{2,1,0:T(8,128)S(1)}, u32[]{:S(2)}, u32[]{:S(2)}) collective-permute-start(f32[16,64,128]{2,1,0:T(8,128)} %get-tuple-element.39), channel_id=1, source_target_pairs={{4,0},{8,4},{12,8},{16,12},{20,16},{24,20},{28,24},{5,1},{9,5},{13... | collective-permute-start | bytes 1572872 | tf_op jit(solution)/shard_map/ppermute | solution.py:653
  36.1 0.7 %collective-permute-done.7.b_ref = f32[65,8,128]{2,1,0:T(8,128)S(1)} collective-permute-done((f32[65,8,128]{2,1,0:T(8,128)S(1)}, f32[65,8,128]{2,1,0:T(8,128)S(1)}, u32[]{:S(2)}, u32[]{:S(2)}) %collective-permute-start.7) | collective-permute-done | bytes 266272 | tf_op jit(solution)/shard_map/ppermute | solution.py:656
  36.8 3.3 %collective-permute-start.8 = (f32[65,8,128]{2,1,0:T(8,128)S(1)}, f32[65,8,128]{2,1,0:T(8,128)S(1)}, u32[]{:S(2)}, u32[]{:S(2)}) collective-permute-start(f32[65,8,128]{2,1,0:T(8,128)S(1)} %add.15.refs_2_.m_high), channel_id=1, source_target_pairs={{0,1},{1,0},{2,3},{3,2},{4,5},{5,4},{6,7},{7,6},{8,9},{9,8},{10,11... | collective-permute-start | bytes 798728 | tf_op jit(solution)/shard_map/ppermute | solution.py:657
  40.1 2.4 %collective-permute-done.4.b_ref = f32[65,8,128]{2,1,0:T(8,128)S(1)} collective-permute-done((f32[65,8,128]{2,1,0:T(8,128)S(1)}, f32[65,8,128]{2,1,0:T(8,128)S(1)}, u32[]{:S(2)}, u32[]{:S(2)}) %collective-permute-start.4) | collective-permute-done | bytes 266272 | tf_op jit(solution)/shard_map/ppermute | solution.py:656
  42.5 1.9 %collective-permute-start.5 = (f32[65,8,128]{2,1,0:T(8,128)S(1)}, f32[65,8,128]{2,1,0:T(8,128)S(1)}, u32[]{:S(2)}, u32[]{:S(2)}) collective-permute-start(f32[65,8,128]{2,1,0:T(8,128)S(1)} %add.14.refs_4_.m_low), channel_id=1, source_target_pairs={{0,1},{1,0},{2,3},{3,2},{4,5},{5,4},{6,7},{7,6},{8,9},{9,8},{10,11... | collective-permute-start | bytes 798728 | tf_op jit(solution)/shard_map/ppermute | solution.py:657
  45.0 0.7 %pad_add_fusion.meta_ref = s32[4]{0:T(128)} fusion(s32[1]{0:T(128)} %bitcast.3, s32[1]{0:T(128)} %bitcast.2, s32[1]{0:T(128)} %bitcast.1, s32[1]{0:T(128)} %bitcast), kind=kLoop, calls=%fused_computation | loop fusion | flops 12 | bytes 32 | tf_op jit(solution)/shard_map/stack | solution.py:633
  45.7 0.0 collective-permute-done.8.refs_3_.o_high
  45.7 0.0 collective-permute-done.5.refs_5_.o_low
  45.7 0.0 collective-permute-done.10.refs_1_
  45.7 0.0 copy-start
  45.7 0.0 copy-start.1
  45.7 7.8 %relax_all.1.before_ref = f32[16,8,16,8,128]{4,3,2,1,0:T(8,128)} custom-call(s32[4]{0:T(128)} %pad_add_fusion.meta_ref, s32[16]{0:T(128)} %sx_ref.5, s32[16]{0:T(128)} %sy_ref.5, f32[16]{0:T(128)} %fx_ref.5, f32[16]{0:T(128)} %fy_ref.5, f32[1]{0:T(128)} %bitcast.13.factor_ref, f32[16,8,16,8,128]{4,3,2,1,0:T(8,128)} %get-tuple-element.36.planes_ref, ...), custom_call_target="tpu_custom_call" | custom-call | tf_op jit(solution)/shard_map/relax_all/pallas_call | solution.py:468
  53.6 3.0 %collective-permute-done.12.refs_1_ = f32[16,64,128]{2,1,0:T(8,128)S(1)} collective-permute-done((f32[16,64,128]{2,1,0:T(8,128)}, f32[16,64,128]{2,1,0:T(8,128)S(1)}, u32[]{:S(2)}, u32[]{:S(2)}) %collective-permute-start.12) | collective-permute-done | bytes 524320 | tf_op jit(solution)/shard_map/ppermute | solution.py:653
  56.5 0.0 collective-permute-done.11.refs_0_
  56.5 0.0 copy-done
  56.5 0.0 copy-done.1
  56.5 5.5 %finish_edges.1 = f32[16,8,16,8,128]{4,3,2,1,0:T(8,128)} custom-call(s32[4]{0:T(128)} %pad_add_fusion.meta_ref, s32[16]{0:T(128)} %sx_ref.5, s32[16]{0:T(128)} %sy_ref.5, f32[16]{0:T(128)} %fx_ref.5, f32[16]{0:T(128)} %fy_ref.5, f32[16]{0:T(128)} %inflow_ref.3, f32[1]{0:T(128)} %bitcast.14.factor_ref, ...), custom_call_target="tpu_custom_call", output_to_operand_aliasing={{}: (12, {})} | custom-call | tf_op jit(solution)/shard_map/finish_edges/pallas_call | solution.py:600
  (5 shorter events, 0.1 us)
Async XLA Ops:
  14.0 3.4 %collective-permute-start.2 = (f32[324,8,128]{2,1,0:T(8,128)S(1)}, f32[324,8,128]{2,1,0:T(8,128)S(1)}, u32[]{:S(2)}, u32[]{:S(2)}) collective-permute-start(f32[324,8,128]{2,1,0:T(8,128)S(1)} %get-tuple-element.31), channel_id=1, source_target_pairs={{0,1},{1,0},{2,3},{3,2},{4,5},{5,4},{6,7},{7,6},{8,9},{9,8},{10,11... | collective-permute-start | bytes 3981320 | tf_op jit(solution)/shard_map/ppermute | solution.py:648
  17.6 13.8 %collective-permute-start.9 = (f32[128,8,128]{2,1,0:T(8,128)S(1)}, f32[128,8,128]{2,1,0:T(8,128)S(1)}, u32[]{:S(2)}, u32[]{:S(2)}) collective-permute-start(f32[128,8,128]{2,1,0:T(8,128)S(1)} %get-tuple-element.37.a_ref), channel_id=1, source_target_pairs={{0,2},{1,3},{2,0},{3,1},{4,6},{5,7},{6,4},{7,5},{8,10},{9,11},{10,... | collective-permute-start | bytes 1572872 | tf_op jit(solution)/shard_map/ppermute | solution.py:656
  18.7 11.4 %collective-permute-start.3 = (f32[36,8,128]{2,1,0:T(8,128)S(1)}, f32[36,8,128]{2,1,0:T(8,128)S(1)}, u32[]{:S(2)}, u32[]{:S(2)}) collective-permute-start(f32[36,8,128]{2,1,0:T(8,128)S(1)} %get-tuple-element.33), channel_id=1, source_target_pairs={{0,4},{4,8},{8,12},{12,16},{16,20},{20,24},{24,28},{1,5},{5,9},{9,... | collective-permute-start | bytes 442376 | tf_op jit(solution)/shard_map/ppermute | solution.py:650
  21.8 7.8 %collective-permute-start.6 = (f32[32,8,128]{2,1,0:T(8,128)S(1)}, f32[32,8,128]{2,1,0:T(8,128)S(1)}, u32[]{:S(2)}, u32[]{:S(2)}) collective-permute-start(f32[32,8,128]{2,1,0:T(8,128)S(1)} %get-tuple-element.35), channel_id=1, source_target_pairs={{4,0},{8,4},{12,8},{16,12},{20,16},{24,20},{28,24},{5,1},{9,5},{13... | collective-permute-start | bytes 393224 | tf_op jit(solution)/shard_map/ppermute | solution.py:651
  25.6 31.0 %collective-permute-start.11 = (f32[16,80,128]{2,1,0:T(8,128)}, f32[16,80,128]{2,1,0:T(8,128)S(1)}, u32[]{:S(2)}, u32[]{:S(2)}) collective-permute-start(f32[16,80,128]{2,1,0:T(8,128)} %get-tuple-element.38), channel_id=1, source_target_pairs={{0,4},{4,8},{8,12},{12,16},{16,20},{20,24},{24,28},{1,5},{5,9},{9,... | collective-permute-start | bytes 1966088 | tf_op jit(solution)/shard_map/ppermute | solution.py:652
  29.7 7.1 %collective-permute-start.7 = (f32[65,8,128]{2,1,0:T(8,128)S(1)}, f32[65,8,128]{2,1,0:T(8,128)S(1)}, u32[]{:S(2)}, u32[]{:S(2)}) collective-permute-start(f32[65,8,128]{2,1,0:T(8,128)S(1)} %join_high.1.a_ref), channel_id=1, source_target_pairs={{0,2},{1,3},{2,0},{3,1},{4,6},{5,7},{6,4},{7,5},{8,10},{9,11},{10,... | collective-permute-start | bytes 798728 | tf_op jit(solution)/shard_map/ppermute | solution.py:656
  30.2 12.3 %collective-permute-start.4 = (f32[65,8,128]{2,1,0:T(8,128)S(1)}, f32[65,8,128]{2,1,0:T(8,128)S(1)}, u32[]{:S(2)}, u32[]{:S(2)}) collective-permute-start(f32[65,8,128]{2,1,0:T(8,128)S(1)} %join_low.1.a_ref), channel_id=1, source_target_pairs={{0,2},{1,3},{2,0},{3,1},{4,6},{5,7},{6,4},{7,5},{8,10},{9,11},{10,... | collective-permute-start | bytes 798728 | tf_op jit(solution)/shard_map/ppermute | solution.py:656
  31.4 14.3 %collective-permute-start.10 = (f32[128,8,128]{2,1,0:T(8,128)S(1)}, f32[128,8,128]{2,1,0:T(8,128)S(1)}, u32[]{:S(2)}, u32[]{:S(2)}) collective-permute-start(f32[128,8,128]{2,1,0:T(8,128)S(1)} %add.16.refs_0_), channel_id=1, source_target_pairs={{0,1},{1,0},{2,3},{3,2},{4,5},{5,4},{6,7},{7,6},{8,9},{9,8},{10,11... | collective-permute-start | bytes 1572872 | tf_op jit(solution)/shard_map/ppermute | solution.py:657
  33.0 23.6 %collective-permute-start.12 = (f32[16,64,128]{2,1,0:T(8,128)}, f32[16,64,128]{2,1,0:T(8,128)S(1)}, u32[]{:S(2)}, u32[]{:S(2)}) collective-permute-start(f32[16,64,128]{2,1,0:T(8,128)} %get-tuple-element.39), channel_id=1, source_target_pairs={{4,0},{8,4},{12,8},{16,12},{20,16},{24,20},{28,24},{5,1},{9,5},{13... | collective-permute-start | bytes 1572872 | tf_op jit(solution)/shard_map/ppermute | solution.py:653
  36.8 8.9 %collective-permute-start.8 = (f32[65,8,128]{2,1,0:T(8,128)S(1)}, f32[65,8,128]{2,1,0:T(8,128)S(1)}, u32[]{:S(2)}, u32[]{:S(2)}) collective-permute-start(f32[65,8,128]{2,1,0:T(8,128)S(1)} %add.15.refs_2_.m_high), channel_id=1, source_target_pairs={{0,1},{1,0},{2,3},{3,2},{4,5},{5,4},{6,7},{7,6},{8,9},{9,8},{10,11... | collective-permute-start | bytes 798728 | tf_op jit(solution)/shard_map/ppermute | solution.py:657
  42.5 3.2 %collective-permute-start.5 = (f32[65,8,128]{2,1,0:T(8,128)S(1)}, f32[65,8,128]{2,1,0:T(8,128)S(1)}, u32[]{:S(2)}, u32[]{:S(2)}) collective-permute-start(f32[65,8,128]{2,1,0:T(8,128)S(1)} %add.14.refs_4_.m_low), channel_id=1, source_target_pairs={{0,1},{1,0},{2,3},{3,2},{4,5},{5,4},{6,7},{7,6},{8,9},{9,8},{10,11... | collective-permute-start | bytes 798728 | tf_op jit(solution)/shard_map/ppermute | solution.py:657
  45.7 10.8 %copy-start = (f32[16,64,128]{2,1,0:T(8,128)S(1)}, f32[16,64,128]{2,1,0:T(8,128)}, u32[]{:S(2)}) copy-start(f32[16,64,128]{2,1,0:T(8,128)} %get-tuple-element.44.refs_3_) | copy-start | bytes 1572868
  45.7 10.8 %copy-start.1 = (f32[16,64,128]{2,1,0:T(8,128)S(1)}, f32[16,64,128]{2,1,0:T(8,128)}, u32[]{:S(2)}) copy-start(f32[16,64,128]{2,1,0:T(8,128)} %get-tuple-element.43.refs_2_) | copy-start | bytes 1572868
where the time goes:
time: 62.4 us; the launch traced here: 62.1 us
  Pallas kernels  27.7 us (44%)
  starting transfers between devices  21.7 us (35%)
  waiting for transfers between devices  10.6 us (17%)
  between operations  1.4 us (2%)
  other arithmetic  0.66 us (1%)
    pallas_call x1, Pallas kernels, advance(): pl.pallas_call(functools.partial(advance_kernel, plan, cuts, group), out_...  14 us
    pallas_call x1, Pallas kernels, relax_all(): pl.pallas_call(functools.partial(relax_kernel, sizes), out_shape=pltpu.HB...  7.84 us
    ppermute x3, starting transfers between devices, total(): return (whole, lax.ppermute(whole, 'vel', partner))  6.73 us
    pallas_call x1, Pallas kernels, finish_edges(): pl.pallas_call(functools.partial(finish_kernel, cuts), out_shape=pltpu.HB...  5.55 us
    ppermute x1, starting transfers between devices, per_device(): from_low = lax.ppermute(up, 'space', forward)  3.11 us
    ppermute x1, starting transfers between devices, per_device(): high_first = lax.ppermute(packs[1], 'space', backward)  3.09 us
    ppermute x1, starting transfers between devices, per_device(): from_high = lax.ppermute(down, 'space', backward)  3.06 us
    ppermute x3, waiting for transfers between devices, total(): lax.ppermute(sums, 'vel', across)  3.05 us
  transfers between devices with their start and end apart: 11, of which 5 were waited for; matrix products, arithmetic and copies ran while one was open for 1% of the time, Pallas kernels for 13%

commit v1 on v0

--- a/solution.py
+++ b/solution.py
@@ -415,7 +415,7 @@
         relax_cells(lambda v: buf[v, k, t], put, values, factor, weights)
 
 
-def relax_kernel(sizes, meta_ref, sx_ref, sy_ref, fx_ref, fy_ref, factor_ref, planes_ref, *refs):
+def relax_kernel(sizes, sx_ref, sy_ref, fx_ref, fy_ref, factor_ref, planes_ref, *refs):
     sums_refs = refs[:-4]
     out_ref, buf, sem_in, sem_out = refs[-4:]
     planes, row_tiles, lane_tiles = planes_ref.shape[:3]
@@ -438,6 +438,7 @@
 
     lax.fori_loop(0, row_tiles, start, 0)
     weights = [velocity(sx_ref, sy_ref, fx_ref, fy_ref, v) for v in range(planes)]
+    core = lax.axis_index("vel") % 2
     begin = 0
     for pair, size in enumerate(sizes):
         sums = sums_refs[2 * pair : 2 * pair + 2]
@@ -447,7 +448,7 @@
             for h in range(2):
                 copy(j, h, False).wait()
                 base = (k - begin) * 4 * half
-                relax_tile(buf, sums, base, meta_ref[3], factor_ref[0], weights, j, h)
+                relax_tile(buf, sums, base, core, factor_ref[0], weights, j, h)
                 copy(j, h, True).start()
             return 0
 
@@ -462,13 +463,13 @@
     lax.fori_loop(0, row_tiles, finish, 0)
 
 
-def relax_all(sizes, meta, small, factor, sums, moved):
+def relax_all(sizes, small, factor, sums, moved):
     planes, row_tiles, lane_tiles = moved.shape[:3]
-    operands = [*in_hbm(meta, *small[:4]), factor, *in_hbm(moved), *sums]
+    operands = [*in_hbm(*small[:4]), factor, *in_hbm(moved), *sums]
     return pl.pallas_call(
         functools.partial(relax_kernel, sizes),
         out_shape=pltpu.HBM(moved.shape, F32),
-        in_specs=[SMEM_SPEC] * 6 + [HBM_SPEC] + [VMEM_SPEC] * len(sums),
+        in_specs=[SMEM_SPEC] * 5 + [HBM_SPEC] + [VMEM_SPEC] * len(sums),
         out_specs=HBM_SPEC,
         scratch_shapes=[
             pltpu.VMEM((planes, row_tiles, lane_tiles, ROW, LANE), F32),
@@ -480,13 +481,13 @@
     )(*operands)
 
 
-def finish_kernel(cuts, meta_ref, sx_ref, sy_ref, fx_ref, fy_ref, inflow_ref, factor_ref, heights_ref,
+def finish_kernel(cuts, sx_ref, sy_ref, fx_ref, fy_ref, inflow_ref, factor_ref, heights_ref,
                   m_low, o_low, m_high, o_high, before_ref, *refs):
     pack_refs = refs[: len(cuts)]
     out_ref, frames, buf, keeps, low_buf, high_buf, bars, sem_in, sem_planes, sem_out = refs[len(cuts) :]
     planes, row_tiles, lane_tiles = before_ref.shape[:3]
     half = lane_tiles // 2
-    row0, first, last, core = (meta_ref[i] for i in range(4))
+    row0, first, last, core = place(row_tiles * ROW)
     needs = [low_need(sy_ref[0]), high_need(sy_ref[0])]
     for v in range(1, planes):
         needs = [needs[0] + low_need(sy_ref[v]), needs[1] + high_need(sy_ref[v])]
@@ -498,8 +499,8 @@
 
     def cases(v):
         shift = sy_ref[v]
-        from_low = (shift >= 0) & (first == 0)
-        return from_low, (shift < 0) & (last == 0), from_low & (shift == CFL)
+        from_low = (shift >= 0) & jnp.logical_not(first)
+        return from_low, (shift < 0) & jnp.logical_not(last), from_low & (shift == CFL)
 
     tile_of = 0, row_tiles - 1, 1
     slot_of = 0, 0, 1
@@ -557,11 +558,16 @@
 
         @pl.when(from_low)
         def _():
-            fill_rows(frames, 0, borders, 8, 16, value)
+            fill_rows(frames, 0, borders, 16, 8, value)
             for t in range(lane_tiles):
-                for r in range(0, 16, ROW):
-                    piece = low_buf[t, pl.ds(low + shift + 1 + r, ROW), :]
-                    frames[0, t + 1, 8 + r : 8 + r + ROW, :] = piece
+                frames[0, t + 1, 16:24, :] = low_buf[t, pl.ds(low + shift + 9, ROW), :]
+
+            @pl.when(shift == CFL)
+            def _():
+                fill_rows(frames, 0, borders, 8, 8, value)
+                for t in range(lane_tiles):
+                    frames[0, t + 1, 8:16, :] = low_buf[t, pl.ds(low + shift + 1, ROW), :]
+
             copy(v, 0, False).wait()
             advect(frames, 0, scalars, [(24, add_masked(v, 0))])
             copy(v, 0, True).start()
@@ -593,14 +599,14 @@
     lax.fori_loop(0, planes, end, 0)
 
 
-def finish_edges(meta, small, factor, heights, sums, packs, cuts, out):
+def finish_edges(small, factor, heights, sums, packs, cuts, out):
     planes, _, lane_tiles = out.shape[:3]
-    fixed = [*in_hbm(meta, *small[:5]), factor, *in_hbm(heights)]
+    fixed = [*in_hbm(*small[:5]), factor, *in_hbm(heights)]
     operands = [*fixed, *sums, *in_hbm(out), *packs]
     return pl.pallas_call(
         functools.partial(finish_kernel, cuts),
         out_shape=pltpu.HBM(out.shape, F32),
-        in_specs=[SMEM_SPEC] * 7 + [VMEM_SPEC] * 5 + [HBM_SPEC] + [ANY_SPEC] * len(cuts),
+        in_specs=[SMEM_SPEC] * 6 + [VMEM_SPEC] * 5 + [HBM_SPEC] + [ANY_SPEC] * len(cuts),
         out_specs=HBM_SPEC,
         scratch_shapes=[
             pltpu.VMEM((2, lane_tiles + 2, 48, LANE), F32),
@@ -624,13 +630,11 @@
     planes, row_count, col_count = populations.shape
     space_count, vel_count = lax.axis_size("space"), lax.axis_size("vel")
     row_tiles, lane_tiles = row_count // ROW, col_count // LANE
-    space, vel = lax.axis_index("space"), lax.axis_index("vel")
     forward = [(i, i + 1) for i in range(space_count - 1)]
     backward = [(target, source) for source, target in forward]
     partner = [(i, i ^ 1) for i in range(vel_count)]
     across = [(i, i ^ 2) for i in range(vel_count)]
 
-    meta = jnp.stack([space * row_count, space == 0, space == space_count - 1, vel % 2]).astype(jnp.int32)
     small = (shift_x, shift_y, frac_x, frac_y, inflow, wall_state)
     factor = impact_frequency_factor.reshape(1)
     bars = heights.reshape(lane_tiles, LANE)
@@ -664,9 +668,9 @@
     sums_low = total(small_call(join_low_kernel, "join_low", edge_low, from_low, (), 1))
     sums_high = total(small_call(join_high_kernel, "join_high", edge_high, from_high, (), 1))
     sizes = len(plan.inside), 2, 2
-    out = relax_all(sizes, meta, small, factor, sums_inside + sums_high + sums_low, moved)
+    out = relax_all(sizes, small, factor, sums_inside + sums_high + sums_low, moved)
     halo = low_first, high_first, *more
-    out = finish_edges(meta, small, factor, bars, sums_low + sums_high, halo, cuts, out)
+    out = finish_edges(small, factor, bars, sums_low + sums_high, halo, cuts, out)
     return out.transpose(0, 1, 3, 2, 4).reshape(planes, row_count, col_count)
 
 

time: 62.4 us -> 62.4 us (level)
  waiting for transfers between devices: 10.6 us -> 11.3 us
  other arithmetic: 0.66 us -> 0 us
    another operation x1 -> x0, other arithmetic: 0.66 us -> none  [per_device(): jnp.stack([space * row_count, space == 0, space == space_count - 1, vel %...]
  transfers between devices with their start and end apart: 11 -> 11, of which waited for: 5 -> 6; matrix products, arithmetic and copies ran while one was open for 1% -> 0% of each run, Pallas kernels for 13% -> 13%
where the time goes in v1:
time: 62.4 us; the launch traced here: 61.8 us
  Pallas kernels  27.2 us (44%)
  starting transfers between devices  21.9 us (35%)
  waiting for transfers between devices  11.3 us (18%)
  between operations  1.4 us (2%)
    pallas_call x1, Pallas kernels, advance(): pl.pallas_call(functools.partial(advance_kernel, plan, cuts, group), out_...  13.8 us
    pallas_call x1, Pallas kernels, relax_all(): pl.pallas_call(functools.partial(relax_kernel, sizes), out_shape=pltpu.HB...  7.8 us
    ppermute x3, starting transfers between devices, total(): return (whole, lax.ppermute(whole, 'vel', partner))  6.73 us
    pallas_call x1, Pallas kernels, finish_edges(): pl.pallas_call(functools.partial(finish_kernel, cuts), out_shape=pltpu.HB...  5.3 us
    ppermute x1, waiting for transfers between devices, per_device(): high_first = lax.ppermute(packs[1], 'space', backward)  3.16 us
    ppermute x1, starting transfers between devices, per_device(): from_low = lax.ppermute(up, 'space', forward)  3.11 us
    ppermute x1, starting transfers between devices, per_device(): high_first = lax.ppermute(packs[1], 'space', backward)  3.09 us
    ppermute x1, starting transfers between devices, per_device(): from_high = lax.ppermute(down, 'space', backward)  3.06 us
  transfers between devices with their start and end apart: 11, of which 6 were waited for; matrix products, arithmetic and copies ran while one was open for 0% of the time, Pallas kernels for 13%

profile of v1, /device:TPU:9, one launch (start us, length us, event | category | flops | bytes accessed | tf_op | source)
XLA Modules:
  0.0 61.8 jit_solution(18255836522628181021)
XLA Ops:
  0.0 13.8 %advance.1 = (f32[16,8,16,8,128]{4,3,2,1,0:T(8,128)}, f32[324,8,128]{2,1,0:T(8,128)S(1)}, f32[324,8,128]{2,1,0:T(8,128)S(1)}, s32[1]{0:T(128)}, f32[16,80,128]{2...) custom-call(s32[16]{0:T(128)} %sx_ref.5, s32[16]{0:T(128)} %sy_ref.5, ...), custom_call_target="tpu_custom_call" | custom-call | tf_op jit(solution)/shard_map/advance/pallas_call | solution.py:302
  13.8 1.1 %collective-permute-start.2 = (f32[324,8,128]{2,1,0:T(8,128)S(1)}, f32[324,8,128]{2,1,0:T(8,128)S(1)}, u32[]{:S(2)}, u32[]{:S(2)}) collective-permute-start(f32[324,8,128]{2,1,0:T(8,128)S(1)} %get-tuple-element.31), channel_id=1, source_target_pairs={{0,1},{1,0},{2,3},{3,2},{4,5},{5,4},{6,7},{7,6},{8,9},{9,8},{10,11... | collective-permute-start | bytes 3981320 | tf_op jit(solution)/shard_map/ppermute | solution.py:652
  14.9 2.7 %collective-permute-done.2.received_ref = f32[324,8,128]{2,1,0:T(8,128)S(1)} collective-permute-done((f32[324,8,128]{2,1,0:T(8,128)S(1)}, f32[324,8,128]{2,1,0:T(8,128)S(1)}, u32[]{:S(2)}, u32[]{:S(2)}) %collective-permute-start.2) | collective-permute-done | bytes 1327136 | tf_op jit(solution)/shard_map/ppermute | solution.py:652
  17.5 0.1 fold.1
  17.7 1.0 %collective-permute-start.9 = (f32[128,8,128]{2,1,0:T(8,128)S(1)}, f32[128,8,128]{2,1,0:T(8,128)S(1)}, u32[]{:S(2)}, u32[]{:S(2)}) collective-permute-start(f32[128,8,128]{2,1,0:T(8,128)S(1)} %get-tuple-element.37.a_ref), channel_id=1, source_target_pairs={{0,2},{1,3},{2,0},{3,1},{4,6},{5,7},{6,4},{7,5},{8,10},{9,11},{10,... | collective-permute-start | bytes 1572872 | tf_op jit(solution)/shard_map/ppermute | solution.py:660
  18.7 3.1 %collective-permute-start.3 = (f32[36,8,128]{2,1,0:T(8,128)S(1)}, f32[36,8,128]{2,1,0:T(8,128)S(1)}, u32[]{:S(2)}, u32[]{:S(2)}) collective-permute-start(f32[36,8,128]{2,1,0:T(8,128)S(1)} %get-tuple-element.33), channel_id=1, source_target_pairs={{0,4},{4,8},{8,12},{12,16},{16,20},{20,24},{24,28},{1,5},{5,9},{9,... | collective-permute-start | bytes 442376 | tf_op jit(solution)/shard_map/ppermute | solution.py:654
  21.8 3.1 %collective-permute-start.6 = (f32[32,8,128]{2,1,0:T(8,128)S(1)}, f32[32,8,128]{2,1,0:T(8,128)S(1)}, u32[]{:S(2)}, u32[]{:S(2)}) collective-permute-start(f32[32,8,128]{2,1,0:T(8,128)S(1)} %get-tuple-element.35), channel_id=1, source_target_pairs={{4,0},{8,4},{12,8},{16,12},{20,16},{24,20},{28,24},{5,1},{9,5},{13... | collective-permute-start | bytes 393224 | tf_op jit(solution)/shard_map/ppermute | solution.py:655
  25.6 2.2 %collective-permute-start.11 = (f32[16,80,128]{2,1,0:T(8,128)}, f32[16,80,128]{2,1,0:T(8,128)S(1)}, u32[]{:S(2)}, u32[]{:S(2)}) collective-permute-start(f32[16,80,128]{2,1,0:T(8,128)} %get-tuple-element.38), channel_id=1, source_target_pairs={{0,4},{4,8},{8,12},{12,16},{16,20},{20,24},{24,28},{1,5},{5,9},{9,... | collective-permute-start | bytes 1966088 | tf_op jit(solution)/shard_map/ppermute | solution.py:656
  27.8 1.9 %collective-permute-done.6.high_ref = f32[32,8,128]{2,1,0:T(8,128)S(1)} collective-permute-done((f32[32,8,128]{2,1,0:T(8,128)S(1)}, f32[32,8,128]{2,1,0:T(8,128)S(1)}, u32[]{:S(2)}, u32[]{:S(2)}) %collective-permute-start.6) | collective-permute-done | bytes 131104 | tf_op jit(solution)/shard_map/ppermute | solution.py:655
  29.7 0.6 collective-permute-start.7
  30.2 0.0 collective-permute-done.3.low_ref
  30.3 1.0 %collective-permute-start.4 = (f32[65,8,128]{2,1,0:T(8,128)S(1)}, f32[65,8,128]{2,1,0:T(8,128)S(1)}, u32[]{:S(2)}, u32[]{:S(2)}) collective-permute-start(f32[65,8,128]{2,1,0:T(8,128)S(1)} %join_low.1.a_ref), channel_id=1, source_target_pairs={{0,2},{1,3},{2,0},{3,1},{4,6},{5,7},{6,4},{7,5},{8,10},{9,11},{10,... | collective-permute-start | bytes 798728 | tf_op jit(solution)/shard_map/ppermute | solution.py:660
  31.3 0.0 collective-permute-done.9.b_ref
  31.3 0.1 add.5.refs_0_
  31.4 1.5 %collective-permute-start.10 = (f32[128,8,128]{2,1,0:T(8,128)S(1)}, f32[128,8,128]{2,1,0:T(8,128)S(1)}, u32[]{:S(2)}, u32[]{:S(2)}) collective-permute-start(f32[128,8,128]{2,1,0:T(8,128)S(1)} %add.5.refs_0_), channel_id=1, source_target_pairs={{0,1},{1,0},{2,3},{3,2},{4,5},{5,4},{6,7},{7,6},{8,9},{9,8},{10,11... | collective-permute-start | bytes 1572872 | tf_op jit(solution)/shard_map/ppermute | solution.py:661
  32.9 3.1 %collective-permute-start.12 = (f32[16,64,128]{2,1,0:T(8,128)}, f32[16,64,128]{2,1,0:T(8,128)S(1)}, u32[]{:S(2)}, u32[]{:S(2)}) collective-permute-start(f32[16,64,128]{2,1,0:T(8,128)} %get-tuple-element.39), channel_id=1, source_target_pairs={{4,0},{8,4},{12,8},{16,12},{20,16},{24,20},{28,24},{5,1},{9,5},{13... | collective-permute-start | bytes 1572872 | tf_op jit(solution)/shard_map/ppermute | solution.py:657
  36.0 0.7 %collective-permute-done.7.b_ref = f32[65,8,128]{2,1,0:T(8,128)S(1)} collective-permute-done((f32[65,8,128]{2,1,0:T(8,128)S(1)}, f32[65,8,128]{2,1,0:T(8,128)S(1)}, u32[]{:S(2)}, u32[]{:S(2)}) %collective-permute-start.7) | collective-permute-done | bytes 266272 | tf_op jit(solution)/shard_map/ppermute | solution.py:660
  36.8 3.3 %collective-permute-start.8 = (f32[65,8,128]{2,1,0:T(8,128)S(1)}, f32[65,8,128]{2,1,0:T(8,128)S(1)}, u32[]{:S(2)}, u32[]{:S(2)}) collective-permute-start(f32[65,8,128]{2,1,0:T(8,128)S(1)} %add.4.refs_2_.m_high), channel_id=1, source_target_pairs={{0,1},{1,0},{2,3},{3,2},{4,5},{5,4},{6,7},{7,6},{8,9},{9,8},{10,11... | collective-permute-start | bytes 798728 | tf_op jit(solution)/shard_map/ppermute | solution.py:661
  40.1 2.4 %collective-permute-done.4.b_ref = f32[65,8,128]{2,1,0:T(8,128)S(1)} collective-permute-done((f32[65,8,128]{2,1,0:T(8,128)S(1)}, f32[65,8,128]{2,1,0:T(8,128)S(1)}, u32[]{:S(2)}, u32[]{:S(2)}) %collective-permute-start.4) | collective-permute-done | bytes 266272 | tf_op jit(solution)/shard_map/ppermute | solution.py:660
  42.5 1.9 %collective-permute-start.5 = (f32[65,8,128]{2,1,0:T(8,128)S(1)}, f32[65,8,128]{2,1,0:T(8,128)S(1)}, u32[]{:S(2)}, u32[]{:S(2)}) collective-permute-start(f32[65,8,128]{2,1,0:T(8,128)S(1)} %add.3.refs_4_.m_low), channel_id=1, source_target_pairs={{0,1},{1,0},{2,3},{3,2},{4,5},{5,4},{6,7},{7,6},{8,9},{9,8},{10,11... | collective-permute-start | bytes 798728 | tf_op jit(solution)/shard_map/ppermute | solution.py:661
  45.0 0.0 collective-permute-done.8.refs_3_.o_high
  45.0 0.5 collective-permute-done.5.refs_5_.o_low
  45.5 0.0 collective-permute-done.10.refs_1_
  45.5 0.0 copy-start
  45.5 0.0 copy-start.1
  45.5 7.8 %relax_all.1.before_ref = f32[16,8,16,8,128]{4,3,2,1,0:T(8,128)} custom-call(s32[16]{0:T(128)} %sx_ref.5, s32[16]{0:T(128)} %sy_ref.5, f32[16]{0:T(128)} %fx_ref.5, f32[16]{0:T(128)} %fy_ref.5, f32[1]{0:T(128)} %bitcast.9.factor_ref, f32[16,8,16,8,128]{4,3,2,1,0:T(8,128)} %get-tuple-element.36.planes_ref, f32[128,8,128]{2,1,0:T(8,128)S(1)} %add.5.refs_0_, ...), custom_call_target="tpu_custom_call" | custom-call | tf_op jit(solution)/shard_map/relax_all/pallas_call | solution.py:469
  53.3 3.2 %collective-permute-done.12.refs_1_ = f32[16,64,128]{2,1,0:T(8,128)S(1)} collective-permute-done((f32[16,64,128]{2,1,0:T(8,128)}, f32[16,64,128]{2,1,0:T(8,128)S(1)}, u32[]{:S(2)}, u32[]{:S(2)}) %collective-permute-start.12) | collective-permute-done | bytes 524320 | tf_op jit(solution)/shard_map/ppermute | solution.py:657
  56.5 0.0 collective-permute-done.11.refs_0_
  56.5 0.0 copy-done
  56.5 0.0 copy-done.1
  56.5 5.3 %finish_edges.1 = f32[16,8,16,8,128]{4,3,2,1,0:T(8,128)} custom-call(s32[16]{0:T(128)} %sx_ref.5, s32[16]{0:T(128)} %sy_ref.5, f32[16]{0:T(128)} %fx_ref.5, f32[16]{0:T(128)} %fy_ref.5, f32[16]{0:T(128)} %inflow_ref.3, f32[1]{0:T(128)} %bitcast.10.factor_ref, s32[16,128]{1,0:T(8,128)} %bitcast.13, ...), custom_call_target="tpu_custom_call", output_to_operand_aliasing={{}: (11, {})} | custom-call | tf_op jit(solution)/shard_map/finish_edges/pallas_call | solution.py:606
  (5 shorter events, 0.1 us)
Async XLA Ops:
  13.8 3.8 %collective-permute-start.2 = (f32[324,8,128]{2,1,0:T(8,128)S(1)}, f32[324,8,128]{2,1,0:T(8,128)S(1)}, u32[]{:S(2)}, u32[]{:S(2)}) collective-permute-start(f32[324,8,128]{2,1,0:T(8,128)S(1)} %get-tuple-element.31), channel_id=1, source_target_pairs={{0,1},{1,0},{2,3},{3,2},{4,5},{5,4},{6,7},{7,6},{8,9},{9,8},{10,11... | collective-permute-start | bytes 3981320 | tf_op jit(solution)/shard_map/ppermute | solution.py:652
  17.7 13.6 %collective-permute-start.9 = (f32[128,8,128]{2,1,0:T(8,128)S(1)}, f32[128,8,128]{2,1,0:T(8,128)S(1)}, u32[]{:S(2)}, u32[]{:S(2)}) collective-permute-start(f32[128,8,128]{2,1,0:T(8,128)S(1)} %get-tuple-element.37.a_ref), channel_id=1, source_target_pairs={{0,2},{1,3},{2,0},{3,1},{4,6},{5,7},{6,4},{7,5},{8,10},{9,11},{10,... | collective-permute-start | bytes 1572872 | tf_op jit(solution)/shard_map/ppermute | solution.py:660
  18.7 11.5 %collective-permute-start.3 = (f32[36,8,128]{2,1,0:T(8,128)S(1)}, f32[36,8,128]{2,1,0:T(8,128)S(1)}, u32[]{:S(2)}, u32[]{:S(2)}) collective-permute-start(f32[36,8,128]{2,1,0:T(8,128)S(1)} %get-tuple-element.33), channel_id=1, source_target_pairs={{0,4},{4,8},{8,12},{12,16},{16,20},{20,24},{24,28},{1,5},{5,9},{9,... | collective-permute-start | bytes 442376 | tf_op jit(solution)/shard_map/ppermute | solution.py:654
  21.8 7.8 %collective-permute-start.6 = (f32[32,8,128]{2,1,0:T(8,128)S(1)}, f32[32,8,128]{2,1,0:T(8,128)S(1)}, u32[]{:S(2)}, u32[]{:S(2)}) collective-permute-start(f32[32,8,128]{2,1,0:T(8,128)S(1)} %get-tuple-element.35), channel_id=1, source_target_pairs={{4,0},{8,4},{12,8},{16,12},{20,16},{24,20},{28,24},{5,1},{9,5},{13... | collective-permute-start | bytes 393224 | tf_op jit(solution)/shard_map/ppermute | solution.py:655
  25.6 31.0 %collective-permute-start.11 = (f32[16,80,128]{2,1,0:T(8,128)}, f32[16,80,128]{2,1,0:T(8,128)S(1)}, u32[]{:S(2)}, u32[]{:S(2)}) collective-permute-start(f32[16,80,128]{2,1,0:T(8,128)} %get-tuple-element.38), channel_id=1, source_target_pairs={{0,4},{4,8},{8,12},{12,16},{16,20},{20,24},{24,28},{1,5},{5,9},{9,... | collective-permute-start | bytes 1966088 | tf_op jit(solution)/shard_map/ppermute | solution.py:656
  29.7 7.1 %collective-permute-start.7 = (f32[65,8,128]{2,1,0:T(8,128)S(1)}, f32[65,8,128]{2,1,0:T(8,128)S(1)}, u32[]{:S(2)}, u32[]{:S(2)}) collective-permute-start(f32[65,8,128]{2,1,0:T(8,128)S(1)} %join_high.1.a_ref), channel_id=1, source_target_pairs={{0,2},{1,3},{2,0},{3,1},{4,6},{5,7},{6,4},{7,5},{8,10},{9,11},{10,... | collective-permute-start | bytes 798728 | tf_op jit(solution)/shard_map/ppermute | solution.py:660
  30.3 12.2 %collective-permute-start.4 = (f32[65,8,128]{2,1,0:T(8,128)S(1)}, f32[65,8,128]{2,1,0:T(8,128)S(1)}, u32[]{:S(2)}, u32[]{:S(2)}) collective-permute-start(f32[65,8,128]{2,1,0:T(8,128)S(1)} %join_low.1.a_ref), channel_id=1, source_target_pairs={{0,2},{1,3},{2,0},{3,1},{4,6},{5,7},{6,4},{7,5},{8,10},{9,11},{10,... | collective-permute-start | bytes 798728 | tf_op jit(solution)/shard_map/ppermute | solution.py:660
  31.4 14.1 %collective-permute-start.10 = (f32[128,8,128]{2,1,0:T(8,128)S(1)}, f32[128,8,128]{2,1,0:T(8,128)S(1)}, u32[]{:S(2)}, u32[]{:S(2)}) collective-permute-start(f32[128,8,128]{2,1,0:T(8,128)S(1)} %add.5.refs_0_), channel_id=1, source_target_pairs={{0,1},{1,0},{2,3},{3,2},{4,5},{5,4},{6,7},{7,6},{8,9},{9,8},{10,11... | collective-permute-start | bytes 1572872 | tf_op jit(solution)/shard_map/ppermute | solution.py:661
  32.9 23.6 %collective-permute-start.12 = (f32[16,64,128]{2,1,0:T(8,128)}, f32[16,64,128]{2,1,0:T(8,128)S(1)}, u32[]{:S(2)}, u32[]{:S(2)}) collective-permute-start(f32[16,64,128]{2,1,0:T(8,128)} %get-tuple-element.39), channel_id=1, source_target_pairs={{4,0},{8,4},{12,8},{16,12},{20,16},{24,20},{28,24},{5,1},{9,5},{13... | collective-permute-start | bytes 1572872 | tf_op jit(solution)/shard_map/ppermute | solution.py:657
  36.8 8.2 %collective-permute-start.8 = (f32[65,8,128]{2,1,0:T(8,128)S(1)}, f32[65,8,128]{2,1,0:T(8,128)S(1)}, u32[]{:S(2)}, u32[]{:S(2)}) collective-permute-start(f32[65,8,128]{2,1,0:T(8,128)S(1)} %add.4.refs_2_.m_high), channel_id=1, source_target_pairs={{0,1},{1,0},{2,3},{3,2},{4,5},{5,4},{6,7},{7,6},{8,9},{9,8},{10,11... | collective-permute-start | bytes 798728 | tf_op jit(solution)/shard_map/ppermute | solution.py:661
  42.5 3.1 %collective-permute-start.5 = (f32[65,8,128]{2,1,0:T(8,128)S(1)}, f32[65,8,128]{2,1,0:T(8,128)S(1)}, u32[]{:S(2)}, u32[]{:S(2)}) collective-permute-start(f32[65,8,128]{2,1,0:T(8,128)S(1)} %add.3.refs_4_.m_low), channel_id=1, source_target_pairs={{0,1},{1,0},{2,3},{3,2},{4,5},{5,4},{6,7},{7,6},{8,9},{9,8},{10,11... | collective-permute-start | bytes 798728 | tf_op jit(solution)/shard_map/ppermute | solution.py:661
  45.5 11.0 %copy-start = (f32[16,64,128]{2,1,0:T(8,128)S(1)}, f32[16,64,128]{2,1,0:T(8,128)}, u32[]{:S(2)}) copy-start(f32[16,64,128]{2,1,0:T(8,128)} %get-tuple-element.44.refs_3_) | copy-start | bytes 1572868
  45.5 11.0 %copy-start.1 = (f32[16,64,128]{2,1,0:T(8,128)S(1)}, f32[16,64,128]{2,1,0:T(8,128)}, u32[]{:S(2)}) copy-start(f32[16,64,128]{2,1,0:T(8,128)} %get-tuple-element.43.refs_2_) | copy-start | bytes 1572868

commit v2 on v1

--- a/solution.py
+++ b/solution.py
@@ -16,7 +16,7 @@
 LANE = 128
 PAD = 16
 F32 = jnp.float32
-LOW_SENT = 80
+LOW_SENT = 72
 HIGH_SENT = 64
 
 SMEM_SPEC = pl.BlockSpec(memory_space=pltpu.SMEM)

time: 62.4 us -> 60.8 us (0.974)
  waiting for transfers between devices: 11.3 us -> 9.89 us
    ppermute x1, waiting for transfers between devices: 3.16 us -> 1.76 us  [per_device(): high_first = lax.ppermute(packs[1], 'space', backward)]
where the time goes in v2:
time: 60.8 us; the launch traced here: 60.4 us
  Pallas kernels  27.4 us (45%)
  starting transfers between devices  21.7 us (36%)
  waiting for transfers between devices  9.89 us (16%)
  between operations  1.4 us (2%)
    pallas_call x1, Pallas kernels, advance(): pl.pallas_call(functools.partial(advance_kernel, plan, cuts, group), out_...  13.9 us
    pallas_call x1, Pallas kernels, relax_all(): pl.pallas_call(functools.partial(relax_kernel, sizes), out_shape=pltpu.HB...  7.8 us
    ppermute x3, starting transfers between devices, total(): return (whole, lax.ppermute(whole, 'vel', partner))  6.73 us
    pallas_call x1, Pallas kernels, finish_edges(): pl.pallas_call(functools.partial(finish_kernel, cuts), out_shape=pltpu.HB...  5.41 us
    ppermute x1, starting transfers between devices, per_device(): from_low = lax.ppermute(up, 'space', forward)  3.11 us
    ppermute x1, starting transfers between devices, per_device(): high_first = lax.ppermute(packs[1], 'space', backward)  3.09 us
    ppermute x3, waiting for transfers between devices, total(): lax.ppermute(sums, 'vel', across)  3.08 us
    ppermute x1, starting transfers between devices, per_device(): from_high = lax.ppermute(down, 'space', backward)  3.06 us
  transfers between devices with their start and end apart: 11, of which 6 were waited for; matrix products, arithmetic and copies ran while one was open for 0% of the time, Pallas kernels for 13%

profile of v2, /device:TPU:9, one launch (start us, length us, event | category | flops | bytes accessed | tf_op | source)
XLA Modules:
  0.0 60.4 jit_solution(11579325996172204182)
XLA Ops:
  0.0 13.9 %advance.1 = (f32[16,8,16,8,128]{4,3,2,1,0:T(8,128)}, f32[324,8,128]{2,1,0:T(8,128)S(1)}, f32[324,8,128]{2,1,0:T(8,128)S(1)}, s32[1]{0:T(128)}, f32[16,72,128]{2...) custom-call(s32[16]{0:T(128)} %sx_ref.5, s32[16]{0:T(128)} %sy_ref.5, ...), custom_call_target="tpu_custom_call" | custom-call | tf_op jit(solution)/shard_map/advance/pallas_call | solution.py:302
  13.9 0.6 %collective-permute-start.2 = (f32[324,8,128]{2,1,0:T(8,128)S(1)}, f32[324,8,128]{2,1,0:T(8,128)S(1)}, u32[]{:S(2)}, u32[]{:S(2)}) collective-permute-start(f32[324,8,128]{2,1,0:T(8,128)S(1)} %get-tuple-element.31), channel_id=1, source_target_pairs={{0,1},{1,0},{2,3},{3,2},{4,5},{5,4},{6,7},{7,6},{8,9},{9,8},{10,11... | collective-permute-start | bytes 3981320 | tf_op jit(solution)/shard_map/ppermute | solution.py:652
  14.5 2.7 %collective-permute-done.2.received_ref = f32[324,8,128]{2,1,0:T(8,128)S(1)} collective-permute-done((f32[324,8,128]{2,1,0:T(8,128)S(1)}, f32[324,8,128]{2,1,0:T(8,128)S(1)}, u32[]{:S(2)}, u32[]{:S(2)}) %collective-permute-start.2) | collective-permute-done | bytes 1327136 | tf_op jit(solution)/shard_map/ppermute | solution.py:652
  17.2 0.1 fold.1
  17.3 1.3 %collective-permute-start.9 = (f32[128,8,128]{2,1,0:T(8,128)S(1)}, f32[128,8,128]{2,1,0:T(8,128)S(1)}, u32[]{:S(2)}, u32[]{:S(2)}) collective-permute-start(f32[128,8,128]{2,1,0:T(8,128)S(1)} %get-tuple-element.37.a_ref), channel_id=1, source_target_pairs={{0,2},{1,3},{2,0},{3,1},{4,6},{5,7},{6,4},{7,5},{8,10},{9,11},{10,... | collective-permute-start | bytes 1572872 | tf_op jit(solution)/shard_map/ppermute | solution.py:660
  18.6 3.1 %collective-permute-start.3 = (f32[36,8,128]{2,1,0:T(8,128)S(1)}, f32[36,8,128]{2,1,0:T(8,128)S(1)}, u32[]{:S(2)}, u32[]{:S(2)}) collective-permute-start(f32[36,8,128]{2,1,0:T(8,128)S(1)} %get-tuple-element.33), channel_id=1, source_target_pairs={{0,4},{4,8},{8,12},{12,16},{16,20},{20,24},{24,28},{1,5},{5,9},{9,... | collective-permute-start | bytes 442376 | tf_op jit(solution)/shard_map/ppermute | solution.py:654
  21.7 3.1 %collective-permute-start.6 = (f32[32,8,128]{2,1,0:T(8,128)S(1)}, f32[32,8,128]{2,1,0:T(8,128)S(1)}, u32[]{:S(2)}, u32[]{:S(2)}) collective-permute-start(f32[32,8,128]{2,1,0:T(8,128)S(1)} %get-tuple-element.35), channel_id=1, source_target_pairs={{4,0},{8,4},{12,8},{16,12},{20,16},{24,20},{28,24},{5,1},{9,5},{13... | collective-permute-start | bytes 393224 | tf_op jit(solution)/shard_map/ppermute | solution.py:655
  25.5 2.2 %collective-permute-start.11 = (f32[16,72,128]{2,1,0:T(8,128)}, f32[16,72,128]{2,1,0:T(8,128)S(1)}, u32[]{:S(2)}, u32[]{:S(2)}) collective-permute-start(f32[16,72,128]{2,1,0:T(8,128)} %get-tuple-element.38), channel_id=1, source_target_pairs={{0,4},{4,8},{8,12},{12,16},{16,20},{20,24},{24,28},{1,5},{5,9},{9,... | collective-permute-start | bytes 1769480 | tf_op jit(solution)/shard_map/ppermute | solution.py:656
  27.7 1.9 %collective-permute-done.6.high_ref = f32[32,8,128]{2,1,0:T(8,128)S(1)} collective-permute-done((f32[32,8,128]{2,1,0:T(8,128)S(1)}, f32[32,8,128]{2,1,0:T(8,128)S(1)}, u32[]{:S(2)}, u32[]{:S(2)}) %collective-permute-start.6) | collective-permute-done | bytes 131104 | tf_op jit(solution)/shard_map/ppermute | solution.py:655
  29.6 0.3 collective-permute-start.7
  29.9 0.0 collective-permute-done.3.low_ref
  29.9 1.3 %collective-permute-start.4 = (f32[65,8,128]{2,1,0:T(8,128)S(1)}, f32[65,8,128]{2,1,0:T(8,128)S(1)}, u32[]{:S(2)}, u32[]{:S(2)}) collective-permute-start(f32[65,8,128]{2,1,0:T(8,128)S(1)} %join_low.1.a_ref), channel_id=1, source_target_pairs={{0,2},{1,3},{2,0},{3,1},{4,6},{5,7},{6,4},{7,5},{8,10},{9,11},{10,... | collective-permute-start | bytes 798728 | tf_op jit(solution)/shard_map/ppermute | solution.py:660
  31.2 0.0 collective-permute-done.9.b_ref
  31.2 0.1 add.5.refs_0_
  31.3 1.5 %collective-permute-start.10 = (f32[128,8,128]{2,1,0:T(8,128)S(1)}, f32[128,8,128]{2,1,0:T(8,128)S(1)}, u32[]{:S(2)}, u32[]{:S(2)}) collective-permute-start(f32[128,8,128]{2,1,0:T(8,128)S(1)} %add.5.refs_0_), channel_id=1, source_target_pairs={{0,1},{1,0},{2,3},{3,2},{4,5},{5,4},{6,7},{7,6},{8,9},{9,8},{10,11... | collective-permute-start | bytes 1572872 | tf_op jit(solution)/shard_map/ppermute | solution.py:661
  32.8 3.1 %collective-permute-start.12 = (f32[16,64,128]{2,1,0:T(8,128)}, f32[16,64,128]{2,1,0:T(8,128)S(1)}, u32[]{:S(2)}, u32[]{:S(2)}) collective-permute-start(f32[16,64,128]{2,1,0:T(8,128)} %get-tuple-element.39), channel_id=1, source_target_pairs={{4,0},{8,4},{12,8},{16,12},{20,16},{24,20},{28,24},{5,1},{9,5},{13... | collective-permute-start | bytes 1572872 | tf_op jit(solution)/shard_map/ppermute | solution.py:657
  35.9 0.7 %collective-permute-done.7.b_ref = f32[65,8,128]{2,1,0:T(8,128)S(1)} collective-permute-done((f32[65,8,128]{2,1,0:T(8,128)S(1)}, f32[65,8,128]{2,1,0:T(8,128)S(1)}, u32[]{:S(2)}, u32[]{:S(2)}) %collective-permute-start.7) | collective-permute-done | bytes 266272 | tf_op jit(solution)/shard_map/ppermute | solution.py:660
  36.7 3.3 %collective-permute-start.8 = (f32[65,8,128]{2,1,0:T(8,128)S(1)}, f32[65,8,128]{2,1,0:T(8,128)S(1)}, u32[]{:S(2)}, u32[]{:S(2)}) collective-permute-start(f32[65,8,128]{2,1,0:T(8,128)S(1)} %add.4.refs_2_.m_high), channel_id=1, source_target_pairs={{0,1},{1,0},{2,3},{3,2},{4,5},{5,4},{6,7},{7,6},{8,9},{9,8},{10,11... | collective-permute-start | bytes 798728 | tf_op jit(solution)/shard_map/ppermute | solution.py:661
  40.0 2.4 %collective-permute-done.4.b_ref = f32[65,8,128]{2,1,0:T(8,128)S(1)} collective-permute-done((f32[65,8,128]{2,1,0:T(8,128)S(1)}, f32[65,8,128]{2,1,0:T(8,128)S(1)}, u32[]{:S(2)}, u32[]{:S(2)}) %collective-permute-start.4) | collective-permute-done | bytes 266272 | tf_op jit(solution)/shard_map/ppermute | solution.py:660
  42.4 1.9 %collective-permute-start.5 = (f32[65,8,128]{2,1,0:T(8,128)S(1)}, f32[65,8,128]{2,1,0:T(8,128)S(1)}, u32[]{:S(2)}, u32[]{:S(2)}) collective-permute-start(f32[65,8,128]{2,1,0:T(8,128)S(1)} %add.3.refs_4_.m_low), channel_id=1, source_target_pairs={{0,1},{1,0},{2,3},{3,2},{4,5},{5,4},{6,7},{7,6},{8,9},{9,8},{10,11... | collective-permute-start | bytes 798728 | tf_op jit(solution)/shard_map/ppermute | solution.py:661
  44.9 0.0 collective-permute-done.8.refs_3_.o_high
  44.9 0.5 collective-permute-done.5.refs_5_.o_low
  45.4 0.0 collective-permute-done.10.refs_1_
  45.4 0.0 copy-start
  45.4 0.0 copy-start.1
  45.4 7.8 %relax_all.1.before_ref = f32[16,8,16,8,128]{4,3,2,1,0:T(8,128)} custom-call(s32[16]{0:T(128)} %sx_ref.5, s32[16]{0:T(128)} %sy_ref.5, f32[16]{0:T(128)} %fx_ref.5, f32[16]{0:T(128)} %fy_ref.5, f32[1]{0:T(128)} %bitcast.9.factor_ref, f32[16,8,16,8,128]{4,3,2,1,0:T(8,128)} %get-tuple-element.36.planes_ref, f32[128,8,128]{2,1,0:T(8,128)S(1)} %add.5.refs_0_, ...), custom_call_target="tpu_custom_call" | custom-call | tf_op jit(solution)/shard_map/relax_all/pallas_call | solution.py:469
  53.3 1.8 %collective-permute-done.12.refs_1_ = f32[16,64,128]{2,1,0:T(8,128)S(1)} collective-permute-done((f32[16,64,128]{2,1,0:T(8,128)}, f32[16,64,128]{2,1,0:T(8,128)S(1)}, u32[]{:S(2)}, u32[]{:S(2)}) %collective-permute-start.12) | collective-permute-done | bytes 524320 | tf_op jit(solution)/shard_map/ppermute | solution.py:657
  55.0 0.0 collective-permute-done.11.refs_0_
  55.0 0.0 copy-done
  55.0 0.0 copy-done.1
  55.0 5.4 %finish_edges.1 = f32[16,8,16,8,128]{4,3,2,1,0:T(8,128)} custom-call(s32[16]{0:T(128)} %sx_ref.5, s32[16]{0:T(128)} %sy_ref.5, f32[16]{0:T(128)} %fx_ref.5, f32[16]{0:T(128)} %fy_ref.5, f32[16]{0:T(128)} %inflow_ref.3, f32[1]{0:T(128)} %bitcast.10.factor_ref, s32[16,128]{1,0:T(8,128)} %bitcast.13, ...), custom_call_target="tpu_custom_call", output_to_operand_aliasing={{}: (11, {})} | custom-call | tf_op jit(solution)/shard_map/finish_edges/pallas_call | solution.py:606
  (5 shorter events, 0.1 us)
Async XLA Ops:
  13.9 3.3 %collective-permute-start.2 = (f32[324,8,128]{2,1,0:T(8,128)S(1)}, f32[324,8,128]{2,1,0:T(8,128)S(1)}, u32[]{:S(2)}, u32[]{:S(2)}) collective-permute-start(f32[324,8,128]{2,1,0:T(8,128)S(1)} %get-tuple-element.31), channel_id=1, source_target_pairs={{0,1},{1,0},{2,3},{3,2},{4,5},{5,4},{6,7},{7,6},{8,9},{9,8},{10,11... | collective-permute-start | bytes 3981320 | tf_op jit(solution)/shard_map/ppermute | solution.py:652
  17.3 13.9 %collective-permute-start.9 = (f32[128,8,128]{2,1,0:T(8,128)S(1)}, f32[128,8,128]{2,1,0:T(8,128)S(1)}, u32[]{:S(2)}, u32[]{:S(2)}) collective-permute-start(f32[128,8,128]{2,1,0:T(8,128)S(1)} %get-tuple-element.37.a_ref), channel_id=1, source_target_pairs={{0,2},{1,3},{2,0},{3,1},{4,6},{5,7},{6,4},{7,5},{8,10},{9,11},{10,... | collective-permute-start | bytes 1572872 | tf_op jit(solution)/shard_map/ppermute | solution.py:660
  18.6 11.3 %collective-permute-start.3 = (f32[36,8,128]{2,1,0:T(8,128)S(1)}, f32[36,8,128]{2,1,0:T(8,128)S(1)}, u32[]{:S(2)}, u32[]{:S(2)}) collective-permute-start(f32[36,8,128]{2,1,0:T(8,128)S(1)} %get-tuple-element.33), channel_id=1, source_target_pairs={{0,4},{4,8},{8,12},{12,16},{16,20},{20,24},{24,28},{1,5},{5,9},{9,... | collective-permute-start | bytes 442376 | tf_op jit(solution)/shard_map/ppermute | solution.py:654
  21.7 7.8 %collective-permute-start.6 = (f32[32,8,128]{2,1,0:T(8,128)S(1)}, f32[32,8,128]{2,1,0:T(8,128)S(1)}, u32[]{:S(2)}, u32[]{:S(2)}) collective-permute-start(f32[32,8,128]{2,1,0:T(8,128)S(1)} %get-tuple-element.35), channel_id=1, source_target_pairs={{4,0},{8,4},{12,8},{16,12},{20,16},{24,20},{28,24},{5,1},{9,5},{13... | collective-permute-start | bytes 393224 | tf_op jit(solution)/shard_map/ppermute | solution.py:655
  25.5 29.5 %collective-permute-start.11 = (f32[16,72,128]{2,1,0:T(8,128)}, f32[16,72,128]{2,1,0:T(8,128)S(1)}, u32[]{:S(2)}, u32[]{:S(2)}) collective-permute-start(f32[16,72,128]{2,1,0:T(8,128)} %get-tuple-element.38), channel_id=1, source_target_pairs={{0,4},{4,8},{8,12},{12,16},{16,20},{20,24},{24,28},{1,5},{5,9},{9,... | collective-permute-start | bytes 1769480 | tf_op jit(solution)/shard_map/ppermute | solution.py:656
  29.6 7.1 %collective-permute-start.7 = (f32[65,8,128]{2,1,0:T(8,128)S(1)}, f32[65,8,128]{2,1,0:T(8,128)S(1)}, u32[]{:S(2)}, u32[]{:S(2)}) collective-permute-start(f32[65,8,128]{2,1,0:T(8,128)S(1)} %join_high.1.a_ref), channel_id=1, source_target_pairs={{0,2},{1,3},{2,0},{3,1},{4,6},{5,7},{6,4},{7,5},{8,10},{9,11},{10,... | collective-permute-start | bytes 798728 | tf_op jit(solution)/shard_map/ppermute | solution.py:660
  29.9 12.4 %collective-permute-start.4 = (f32[65,8,128]{2,1,0:T(8,128)S(1)}, f32[65,8,128]{2,1,0:T(8,128)S(1)}, u32[]{:S(2)}, u32[]{:S(2)}) collective-permute-start(f32[65,8,128]{2,1,0:T(8,128)S(1)} %join_low.1.a_ref), channel_id=1, source_target_pairs={{0,2},{1,3},{2,0},{3,1},{4,6},{5,7},{6,4},{7,5},{8,10},{9,11},{10,... | collective-permute-start | bytes 798728 | tf_op jit(solution)/shard_map/ppermute | solution.py:660
  31.3 14.2 %collective-permute-start.10 = (f32[128,8,128]{2,1,0:T(8,128)S(1)}, f32[128,8,128]{2,1,0:T(8,128)S(1)}, u32[]{:S(2)}, u32[]{:S(2)}) collective-permute-start(f32[128,8,128]{2,1,0:T(8,128)S(1)} %add.5.refs_0_), channel_id=1, source_target_pairs={{0,1},{1,0},{2,3},{3,2},{4,5},{5,4},{6,7},{7,6},{8,9},{9,8},{10,11... | collective-permute-start | bytes 1572872 | tf_op jit(solution)/shard_map/ppermute | solution.py:661
  32.8 22.2 %collective-permute-start.12 = (f32[16,64,128]{2,1,0:T(8,128)}, f32[16,64,128]{2,1,0:T(8,128)S(1)}, u32[]{:S(2)}, u32[]{:S(2)}) collective-permute-start(f32[16,64,128]{2,1,0:T(8,128)} %get-tuple-element.39), channel_id=1, source_target_pairs={{4,0},{8,4},{12,8},{16,12},{20,16},{24,20},{28,24},{5,1},{9,5},{13... | collective-permute-start | bytes 1572872 | tf_op jit(solution)/shard_map/ppermute | solution.py:657
  36.7 8.2 %collective-permute-start.8 = (f32[65,8,128]{2,1,0:T(8,128)S(1)}, f32[65,8,128]{2,1,0:T(8,128)S(1)}, u32[]{:S(2)}, u32[]{:S(2)}) collective-permute-start(f32[65,8,128]{2,1,0:T(8,128)S(1)} %add.4.refs_2_.m_high), channel_id=1, source_target_pairs={{0,1},{1,0},{2,3},{3,2},{4,5},{5,4},{6,7},{7,6},{8,9},{9,8},{10,11... | collective-permute-start | bytes 798728 | tf_op jit(solution)/shard_map/ppermute | solution.py:661
  42.4 3.1 %collective-permute-start.5 = (f32[65,8,128]{2,1,0:T(8,128)S(1)}, f32[65,8,128]{2,1,0:T(8,128)S(1)}, u32[]{:S(2)}, u32[]{:S(2)}) collective-permute-start(f32[65,8,128]{2,1,0:T(8,128)S(1)} %add.3.refs_4_.m_low), channel_id=1, source_target_pairs={{0,1},{1,0},{2,3},{3,2},{4,5},{5,4},{6,7},{7,6},{8,9},{9,8},{10,11... | collective-permute-start | bytes 798728 | tf_op jit(solution)/shard_map/ppermute | solution.py:661
  45.4 9.6 %copy-start = (f32[16,72,128]{2,1,0:T(8,128)S(1)}, f32[16,72,128]{2,1,0:T(8,128)}, u32[]{:S(2)}) copy-start(f32[16,72,128]{2,1,0:T(8,128)} %get-tuple-element.43.refs_2_) | copy-start | bytes 1769476
  45.4 9.6 %copy-start.1 = (f32[16,64,128]{2,1,0:T(8,128)S(1)}, f32[16,64,128]{2,1,0:T(8,128)}, u32[]{:S(2)}) copy-start(f32[16,64,128]{2,1,0:T(8,128)} %get-tuple-element.44.refs_3_) | copy-start | bytes 1572868
